TPU v7x, 256 devices: a whole 4x4x8 slice. The times are simulated.
256 devices in a mesh: order: 16 (over x, y), lat: 16 (over z, core).
Axes of the slice: x: 4, y: 4, z: 8, core: 2. Of those that a mesh axis runs over, the one named last changes fastest.
Arguments:
- fourier: bfloat16 [512, 64, 2048], P('order', None, 'lat'), may hold values from -6 to 6
- quad_weights: float32 [2048], P('lat'), may hold values from 0.5 to 1.5
- leaf_basis: bfloat16 [512, 64, 2048], P('order', None, 'lat'), may hold values from -0.5 to 0.5
- level_factors: bfloat16 [512, 4, 2, 16, 64, 64], P('order', None, None, 'lat'), may hold values from -0.5 to 0.5
- sparsity: int32 [512, 4, 16], P('order', None, 'lat'), may hold values 0 or 1
- root_basis: bfloat16 [512, 64, 2048], P(None, None, 'lat'), may hold values from -0.75 to 0.75
- order_of_slot: int32 [512], replicated, may hold values from 0 to 511, each once
Outputs:
- spectra: bfloat16 [32, 2, 2048, 512], P('order', None, 'lat')
Inputs may be any that keep to these rules, and one draw needn't show every extreme that they name: `order_of_slot`: every window index appears in exactly one slot.
All inputs are finite; a program needn't handle non-finite values. No bound on the sum of `sparsity` on one device may be relied on, other than what follows from the above.
Results may differ from a plain program's by a relative error of at most 0.0081.
Values may be sent and summed in bfloat16 or wider, within the bound.
A program may use at most 64 MiB of HBM per device.

v0:
```python
import jax
import jax.numpy as jnp
from jax import lax
from jax.sharding import PartitionSpec as P

DEGREES = 2048


def partner_2(array, axis, bit):
    return lax.ppermute(array, axis, [(i, i ^ 1 << bit) for i in range(lax.axis_size(axis))])


def per_device(
    fourier, quad_weights, leaf_basis, level_factors, sparsity, root_basis, order_of_slot
):
    weighted = (fourier.astype(jnp.float32) * quad_weights[None, None, :]).astype(jnp.bfloat16)
    rank_state = jnp.einsum(
        "orj,ocj->orc", leaf_basis, weighted, preferred_element_type=jnp.float32
    ).astype(jnp.bfloat16)
    depth_count = level_factors.shape[1]
    for depth_bit in range(depth_count):
        partner = partner_2(rank_state, "lat", depth_bit)
        own_term = jnp.einsum(
            "ors,osc->orc",
            level_factors[:, depth_bit, 0, 0],
            rank_state,
            preferred_element_type=jnp.float32,
        )
        cross_term = jnp.einsum(
            "ors,osc->orc",
            level_factors[:, depth_bit, 1, 0],
            partner,
            preferred_element_type=jnp.float32,
        )
        present = sparsity[:, depth_bit, 0].astype(jnp.float32)[:, None, None]
        rank_state = (own_term + present * cross_term).astype(jnp.bfloat16)
    slot_local = fourier.shape[0]
    first_slot = lax.axis_index("order") * slot_local
    local_root = lax.dynamic_slice_in_dim(root_basis, first_slot, slot_local, 0)
    coefficient = jnp.einsum(
        "orl,orc->olc", local_root, rank_state, preferred_element_type=jnp.float32
    ).astype(jnp.bfloat16)
    arrived = lax.all_to_all(coefficient, "order", split_axis=2, concat_axis=0, tiled=True)
    slot_count = order_of_slot.shape[0]
    inverse = (
        jnp.zeros((slot_count,), jnp.int32)
        .at[order_of_slot]
        .set(jnp.arange(slot_count, dtype=jnp.int32))
    )
    natural = jnp.take(arrived, inverse, axis=0)
    degree_local = arrived.shape[1]
    columns = arrived.shape[2]
    degree = lax.axis_index("lat") * degree_local + jnp.arange(degree_local, dtype=jnp.int32)
    window = DEGREES // slot_count * jnp.arange(slot_count, dtype=jnp.int32)
    alive_mask = degree[None, :, None] >= window[:, None, None]
    masked = jnp.where(alive_mask, natural, jnp.zeros((), natural.dtype))
    return masked.reshape(slot_count, degree_local, columns // 2, 2).transpose(2, 3, 1, 0)


def solution(mesh):
    return jax.shard_map(
        per_device,
        mesh=mesh,
        in_specs=(
            P("order", None, "lat"),
            P("lat"),
            P("order", None, "lat"),
            P("order", None, None, "lat", None, None),
            P("order", None, "lat"),
            P(None, None, "lat"),
            P(),
        ),
        out_specs=P("order", None, "lat", None),
        check_vma=False,
    )
```

profile of v0, /device:TPU:8, one launch (start us, length us, event | category | flops | bytes accessed | tf_op | source)
XLA Modules:
  0.0 104.5 jit_solution(12461444689542616690)
XLA Ops:
  0.0 1.0 copy-done
  1.0 1.4 %convolution_convert_fusion.1 = bf16[32,64,64]{2,1,0:T(8,128)(2,1)S(1)} fusion(bf16[32,64,128]{2,1,0:T(8,128)(2,1)S(1)} %copy-done, bf16[32,64,128]{2,1,0:T(8,128)(2,1)} %param.7, f32[128]{0:T(128)} %param.8), kind=kOutput, calls=%fused_computation.15 | convolution fusion | flops 34471936 | bytes 1311232 | tf_op jit(solution)/shard_map/orj,ocj->orc/dot_general | solution.py:17
  2.6 0.7 convert_bitcast_fusion
  3.3 0.7 compare_select_fusion.1
  4.0 2.4 %scatter_custom_fusion = s32[512]{0:T(512)S(1)} fusion(s32[512]{0:T(512)S(1)} %compare_select_fusion.1, s32[512]{0:T(512)S(1)} %iota.15, s32[]{:T(128)} %constant.13.clone.1), kind=kCustom, calls=%fused_computation.47 | custom fusion | bytes 2052 | tf_op jit(solution)/shard_map/scatter | solution.py:48
  6.5 1.6 %fusion.19 = f32[32,64,64]{2,1,0:T(8,128)S(1)} fusion(bf16[32,64,64]{2,1,0:T(8,128)(2,1)S(1)} %convolution_convert_fusion.1, bf16[32,4,2,1,64,64]{5,4,3,2,1,0:T(8,128)(2,1)} %param.10), kind=kOutput, calls=%fused_computation.27 | convolution fusion | flops 16777216 | bytes 1310720 | tf_op jit(solution)/shard_map/ors,osc->orc/dot_general | solution.py:23
  8.1 1.5 %fusion.4 = bf16[32,64,64]{2,1,0:T(8,128)(2,1)S(1)} fusion(f32[32,64,64]{2,1,0:T(8,128)S(1)} %fusion.19, bf16[32,64,64]{1,2,0:T(8,128)(2,1)S(1)} %collective-permute-done, bf16[32,4,2,1,64,64]{5,4,3,2,1,0:T(8,128)(2,1)} %param.10, f32[32]{0:T(128)S(1)} %get-tuple-element.7), kind=kOutput, calls=%fused_computation.10 | convolution fusion | flops 17170432 | bytes 1572992 | tf_op jit(solution)/shard_map/ors,osc->orc/dot_general | solution.py:29
  9.6 2.0 %collective-permute-start.1 = (bf16[32,64,64]{1,2,0:T(8,128)(2,1)S(1)}, bf16[32,64,64]{1,2,0:T(8,128)(2,1)S(1)}, u32[]{:S(2)}, u32[]{:S(2)}) collective-permute-start(bf16[32,64,64]{1,2,0:T(8,128)(2,1)S(1)} %bitcast.73), channel_id=1, source_target_pairs={{0,2},{1,3},{2,0},{3,1},{4,6},{5,7},{6,4},{7,5},{8,10},{9,11},{10,... | collective-permute-start | bytes 786440 | tf_op jit(solution)/shard_map/ppermute | solution.py:10
  11.6 0.4 fusion.16
  12.0 12.2 %collective-permute-done.1 = bf16[32,64,64]{1,2,0:T(8,128)(2,1)S(1)} collective-permute-done((bf16[32,64,64]{1,2,0:T(8,128)(2,1)S(1)}, bf16[32,64,64]{1,2,0:T(8,128)(2,1)S(1)}, u32[]{:S(2)}, u32[]{:S(2)}) %collective-permute-start.1) | collective-permute-done | bytes 262176 | tf_op jit(solution)/shard_map/ppermute | solution.py:10
  24.1 0.4 fusion.5
  24.5 3.4 %collective-permute-start.2 = (bf16[32,64,64]{1,2,0:T(8,128)(2,1)S(1)}, bf16[32,64,64]{1,2,0:T(8,128)(2,1)S(1)}, u32[]{:S(2)}, u32[]{:S(2)}) collective-permute-start(bf16[32,64,64]{1,2,0:T(8,128)(2,1)S(1)} %bitcast.74), channel_id=1, source_target_pairs={{0,4},{1,5},{2,6},{3,7},{4,0},{5,1},{6,2},{7,3},{8,12},{9,13},{10,... | collective-permute-start | bytes 786440 | tf_op jit(solution)/shard_map/ppermute | solution.py:10
  28.3 22.7 %collective-permute-done.2 = bf16[32,64,64]{1,2,0:T(8,128)(2,1)S(1)} collective-permute-done((bf16[32,64,64]{1,2,0:T(8,128)(2,1)S(1)}, bf16[32,64,64]{1,2,0:T(8,128)(2,1)S(1)}, u32[]{:S(2)}, u32[]{:S(2)}) %collective-permute-start.2) | collective-permute-done | bytes 262176 | tf_op jit(solution)/shard_map/ppermute | solution.py:10
  51.0 0.4 fusion.6
  51.4 6.4 %collective-permute-start.3 = (bf16[32,64,64]{1,2,0:T(8,128)(2,1)S(1)}, bf16[32,64,64]{1,2,0:T(8,128)(2,1)S(1)}, u32[]{:S(2)}, u32[]{:S(2)}) collective-permute-start(bf16[32,64,64]{1,2,0:T(8,128)(2,1)S(1)} %bitcast.75), channel_id=1, source_target_pairs={{0,8},{1,9},{2,10},{3,11},{4,12},{5,13},{6,14},{7,15},{8,0},{9,1},... | collective-permute-start | bytes 786440 | tf_op jit(solution)/shard_map/ppermute | solution.py:10
  58.2 22.6 %collective-permute-done.3 = bf16[32,64,64]{1,2,0:T(8,128)(2,1)S(1)} collective-permute-done((bf16[32,64,64]{1,2,0:T(8,128)(2,1)S(1)}, bf16[32,64,64]{1,2,0:T(8,128)(2,1)S(1)}, u32[]{:S(2)}, u32[]{:S(2)}) %collective-permute-start.3) | collective-permute-done | bytes 262176 | tf_op jit(solution)/shard_map/ppermute | solution.py:10
  80.8 1.8 %convolution_convert_fusion = bf16[32,128,64]{1,2,0:T(8,128)(2,1)S(1)} fusion(f32[32,64,64]{2,1,0:T(8,128)S(1)} %fusion.10, bf16[32,64,64]{1,2,0:T(8,128)(2,1)S(1)} %collective-permute-done.3, bf16[32,4,2,1,64,64]{5,4,3,2,1,0:T(8,128)(2,1)} %param.10, f32[32]{0:T(128)S(1)} %get-tuple-element.5, bf16[512,64,128]{2,1,0:T(8,128)(2,1)} %param.12, s32[]{:T(128)S(6)} %select_n.23), kind=kOutput, calls=%fused_computation.14 | convolution fusion | flops 50987008 | bytes 2359428 | tf_op jit(solution)/shard_map/orl,orc->olc/dot_general | solution.py:40
  82.6 1.1 %copy.42 = bf16[32,128,64]{1,0,2:T(8,128)(2,1)} copy(bf16[32,128,64]{1,2,0:T(8,128)(2,1)S(1)} %convolution_convert_fusion) | data formatting | bytes 1048576 | tf_op jit(solution)/shard_map/convert_element_type | solution.py:42
  83.7 7.4 %all-to-all-start = ((bf16[32,128,64]{1,0,2:T(8,128)(2,1)}), bf16[32,128,64]{1,0,2:T(8,128)(2,1)S(1)}, u32[]{:S(2)}, u32[]{:S(2)}) async-start(bf16[32,128,64]{1,0,2:T(8,128)(2,1)} %copy.42), calls=%async_computation | async-start | bytes 1048576 | tf_op jit(solution)/shard_map/all_to_all | solution.py:43
  91.2 9.0 %all-to-all-done = bf16[32,128,64]{1,0,2:T(8,128)(2,1)S(1)} async-done(((bf16[32,128,64]{1,0,2:T(8,128)(2,1)}), bf16[32,128,64]{1,0,2:T(8,128)(2,1)S(1)}, u32[]{:S(2)}, u32[]{:S(2)}) %all-to-all-start) | async-done | bytes 524320 | tf_op jit(solution)/shard_map/all_to_all | solution.py:43
  100.3 0.4 copy.44
  100.7 2.1 %gather_fusion = bf16[512,128,4]{1,2,0:T(4,128)(2,1)S(1)} fusion(bf16[512,128,4]{1,2,0:T(4,128)(2,1)S(1)} %copy.44, s32[1024]{0:T(1024)S(1)} %pad_clamp_fusion), kind=kCustom, calls=%fused_computation | custom fusion | bytes 1050624 | tf_op jit(solution)/shard_map/jit(_take)/gather | solution.py:50
  102.8 0.7 copy.45
  103.6 0.9 select_bitcast_fusion
  (15 shorter events, 1.1 us)
Async XLA Ops:
  0.0 1.0 copy-start
  2.5 5.6 %collective-permute-start = (bf16[32,64,64]{1,2,0:T(8,128)(2,1)S(1)}, bf16[32,64,64]{1,2,0:T(8,128)(2,1)S(1)}, u32[]{:S(2)}, u32[]{:S(2)}) collective-permute-start(bf16[32,64,64]{1,2,0:T(8,128)(2,1)S(1)} %bitcast.72), channel_id=1, source_target_pairs={{0,1},{1,0},{2,3},{3,2},{4,5},{5,4},{6,7},{7,6},{8,9},{9,8},{10,11... | collective-permute-start | bytes 786440 | tf_op jit(solution)/shard_map/ppermute | solution.py:10
  6.5 5.1 %copy-start.1 = (bf16[32,4,2,1,64,64]{5,4,3,2,1,0:T(8,128)(2,1)S(1)}, bf16[32,4,2,1,64,64]{5,4,3,2,1,0:T(8,128)(2,1)}, u32[]{:S(2)}) copy-start(bf16[32,4,2,1,64,64]{5,4,3,2,1,0:T(8,128)(2,1)} %param.10) | copy-start | bytes 6291460
  9.6 14.6 %collective-permute-start.1 = (bf16[32,64,64]{1,2,0:T(8,128)(2,1)S(1)}, bf16[32,64,64]{1,2,0:T(8,128)(2,1)S(1)}, u32[]{:S(2)}, u32[]{:S(2)}) collective-permute-start(bf16[32,64,64]{1,2,0:T(8,128)(2,1)S(1)} %bitcast.73), channel_id=1, source_target_pairs={{0,2},{1,3},{2,0},{3,1},{4,6},{5,7},{6,4},{7,5},{8,10},{9,11},{10,... | collective-permute-start | bytes 786440 | tf_op jit(solution)/shard_map/ppermute | solution.py:10
  24.5 26.5 %collective-permute-start.2 = (bf16[32,64,64]{1,2,0:T(8,128)(2,1)S(1)}, bf16[32,64,64]{1,2,0:T(8,128)(2,1)S(1)}, u32[]{:S(2)}, u32[]{:S(2)}) collective-permute-start(bf16[32,64,64]{1,2,0:T(8,128)(2,1)S(1)} %bitcast.74), channel_id=1, source_target_pairs={{0,4},{1,5},{2,6},{3,7},{4,0},{5,1},{6,2},{7,3},{8,12},{9,13},{10,... | collective-permute-start | bytes 786440 | tf_op jit(solution)/shard_map/ppermute | solution.py:10
  51.4 29.4 %collective-permute-start.3 = (bf16[32,64,64]{1,2,0:T(8,128)(2,1)S(1)}, bf16[32,64,64]{1,2,0:T(8,128)(2,1)S(1)}, u32[]{:S(2)}, u32[]{:S(2)}) collective-permute-start(bf16[32,64,64]{1,2,0:T(8,128)(2,1)S(1)} %bitcast.75), channel_id=1, source_target_pairs={{0,8},{1,9},{2,10},{3,11},{4,12},{5,13},{6,14},{7,15},{8,0},{9,1},... | collective-permute-start | bytes 786440 | tf_op jit(solution)/shard_map/ppermute | solution.py:10
  83.7 16.6 %all-to-all-start = ((bf16[32,128,64]{1,0,2:T(8,128)(2,1)}), bf16[32,128,64]{1,0,2:T(8,128)(2,1)S(1)}, u32[]{:S(2)}, u32[]{:S(2)}) async-start(bf16[32,128,64]{1,0,2:T(8,128)(2,1)} %copy.42), calls=%async_computation | async-start | bytes 1048576 | tf_op jit(solution)/shard_map/all_to_all | solution.py:43
where the time goes:
time: 105 us; the launch traced here: 104 us
  waiting for transfers between devices  66.6 us (63%)
  starting transfers between devices  19.2 us (18%)
  matrix products  8.23 us (8%)
  local copies, waits for them, and re-layouts  7.89 us (8%)
  other arithmetic  2.42 us (2%)
    ppermute x4, waiting for transfers between devices, partner_2(): lax.ppermute(array, axis, [(i, i ^ 1 << bit) for i in range(lax.axis_size...  57.5 us
    ppermute x4, starting transfers between devices, partner_2(): lax.ppermute(array, axis, [(i, i ^ 1 << bit) for i in range(lax.axis_size...  11.8 us
    all_to_all x1, waiting for transfers between devices, per_device(): lax.all_to_all(coefficient, 'order', split_axis=2, concat_axis=0, tiled=T...  9.03 us
    all_to_all x1, starting transfers between devices, per_device(): lax.all_to_all(coefficient, 'order', split_axis=2, concat_axis=0, tiled=T...  7.39 us
    gather x2, local copies, waits for them, and re-layouts, per_device(): natural = jnp.take(arrived, inverse, axis=0)  2.83 us
    dot_general x4, matrix products, per_device(): jnp.einsum('ors,osc->orc', level_factors[:, depth_bit, 0, 0], rank_state,...  2.77 us
    scatter x1, local copies, waits for them, and re-layouts, per_device(): inverse = jnp.zeros((slot_count,), jnp.int32).at[order_of_slot].set(jnp.a...  2.43 us
    dot_general x3, matrix products, per_device(): jnp.einsum('ors,osc->orc', level_factors[:, depth_bit, 1, 0], partner, pr...  2.27 us
  transfers between devices with their start and end apart: 5, of which 4 were waited for; matrix products, arithmetic and copies ran while one was open for 6% of the time, Pallas kernels for 0%

commit v1 on v0

v1 whole, which is shorter than its diff:
```python
import functools

import jax
import jax.numpy as jnp
from jax import lax
from jax.experimental import pallas as pl
from jax.experimental.pallas import tpu as pltpu
from jax.sharding import PartitionSpec as P

DEGREES = 2048
MESH = pl.DeviceIdType.MESH
BF16 = jnp.bfloat16
F32 = jnp.float32
I32 = jnp.int32

SLOTS = 32
CHUNK = 4
CHUNKS = SLOTS // CHUNK
LEVELS = 4
GROUPS = 4
N_ORDER = 16
RANK = 64


def schedule():
    events = []
    keyed = []
    for c in range(CHUNKS):
        keyed.append((c * 1.0, 0, ("s", 0, c)))
        keyed.append((c * 1.0 + 2.5, 1, ("s", 1, c)))
        keyed.append((c * 1.0 + 5.5, 2, ("s", 2, c)))
        keyed.append((c * 2.0 + 12.0, 3, ("s", 3, c)))
        keyed.append((c * 2.0 + 18.5, 4, ("s", 4, c)))
    for g in range(GROUPS):
        keyed.append(((2 * g + 1) * 2.0 + 18.6, 5, ("a", g)))
        keyed.append(((2 * g + 1) * 2.0 + 18.6 + 3.5, 6, ("r", g)))
    keyed.append((8.1, 7, ("p",)))
    for _, _, event in sorted(keyed):
        events.append(event)
    return events


def kernel(
    four_hbm, quad_hbm, leaf_hbm, fac_hbm, spars_hbm, root_hbm, order_hbm, out_hbm,
    four, quad, leaf, fac, spars, root, order, out,
    state, partner, own, perm, send_buf, recv_buf, order_col, pick, coef, coef_t,
    in_sem, small_sem, root_sem, out_sem, send_sem, recv_sem, a2a_send_sem, a2a_recv_sem,
):
    me_o = lax.axis_index("order")
    me_l = lax.axis_index("lat")
    peers = [me_l ^ (1 << k) for k in range(LEVELS)]

    def loads(c):
        span = pl.ds(c * CHUNK, CHUNK)
        return [
            pltpu.make_async_copy(four_hbm.at[span], four.at[span], in_sem.at[0, c]),
            pltpu.make_async_copy(leaf_hbm.at[span], leaf.at[span], in_sem.at[1, c]),
            pltpu.make_async_copy(fac_hbm.at[span, :, :, 0], fac.at[span], in_sem.at[2, c]),
        ]

    small = [
        pltpu.make_async_copy(quad_hbm, quad, small_sem.at[0]),
        pltpu.make_async_copy(spars_hbm, spars, small_sem.at[1]),
        pltpu.make_async_copy(order_hbm, order, small_sem.at[2]),
    ]
    root_copy = pltpu.make_async_copy(root_hbm, root, root_sem)
    all_loads = [loads(c) for c in range(CHUNKS)]
    for copy in small:
        copy.start()
    for c in range(CHUNKS):
        for copy in all_loads[c]:
            copy.start()
    root_copy.start()

    barrier = pltpu.get_barrier_semaphore()
    for peer in peers:
        pl.semaphore_signal(barrier, inc=1, device_id=(me_o, peer), device_id_type=MESH)
    for i in range(1, N_ORDER):
        pl.semaphore_signal(
            barrier, inc=1, device_id=(lax.rem(me_o + i, N_ORDER), me_l), device_id_type=MESH
        )

    def level_copy(k, c):
        return pltpu.make_async_remote_copy(
            src_ref=state.at[k, c],
            dst_ref=partner.at[k, c],
            send_sem=send_sem.at[k, c],
            recv_sem=recv_sem.at[k, c],
            device_id=(me_o, peers[k]),
            device_id_type=MESH,
        )

    def a2a_copy(g, dest, source):
        return pltpu.make_async_remote_copy(
            src_ref=send_buf.at[g, dest],
            dst_ref=recv_buf.at[g, source],
            send_sem=a2a_send_sem.at[g, dest],
            recv_sem=a2a_recv_sem.at[g, source],
            device_id=(dest, me_l),
            device_id_type=MESH,
        )

    low = lax.broadcasted_iota(I32, (RANK, 128), 1) < RANK

    def both(a, b):
        return jnp.concatenate([a, b], axis=0)

    def diagonal(product):
        return jnp.where(low, product[:RANK], product[RANK:])

    def own_terms(k, c):
        for h in range(2):
            s0, s1 = c * CHUNK + h, c * CHUNK + 2 + h
            a = both(fac[s0, k, 0], fac[s1, k, 0])
            own[k, c, h] = diagonal(jnp.dot(a, state[k, c, h], preferred_element_type=F32))

    def start_event(c):
        for copy in all_loads[c][:2]:
            copy.wait()
        w = quad[...]
        for h in range(2):
            s0, s1 = c * CHUNK + h, c * CHUNK + 2 + h
            weighted = both(
                (four[s0].astype(F32) * w).astype(BF16), (four[s1].astype(F32) * w).astype(BF16)
            )
            basis = both(leaf[s0], leaf[s1])
            product = lax.dot_general(
                basis, weighted, (((1,), (1,)), ((), ())), preferred_element_type=F32
            )
            state[0, c, h] = diagonal(product).astype(BF16)

    def level_event(k, c):
        level_copy(k, c).wait_recv()
        for h in range(2):
            s0, s1 = c * CHUNK + h, c * CHUNK + 2 + h
            b = both(fac[s0, k, 1], fac[s1, k, 1])
            cross = diagonal(jnp.dot(b, partner[k, c, h], preferred_element_type=F32))
            present = jnp.where(low, spars[k, 0, s0], spars[k, 0, s1]).astype(F32)
            state[k + 1, c, h] = (own[k, c, h] + present * cross).astype(BF16)

    def a2a_event(g):
        x = jnp.concatenate(
            [
                state[LEVELS, 2 * g].reshape(2 * RANK, 128),
                state[LEVELS, 2 * g + 1].reshape(2 * RANK, 128),
            ],
            axis=1,
        )
        packed = lax.dot_general(
            perm[...], x, (((1,), (1,)), ((), ())), preferred_element_type=F32
        ).astype(BF16)
        send_buf[g] = packed.reshape(N_ORDER, 16, 128)

        def one(i, carry):
            a2a_copy(g, lax.rem(me_o + i, N_ORDER), me_o).start()
            return carry

        lax.fori_loop(1, N_ORDER, one, 0)
        recv_buf[g, me_o] = send_buf[g, me_o]

    def prepare_perm():
        row = lax.broadcasted_iota(I32, (256, 256), 0)
        col = lax.broadcasted_iota(I32, (256, 256), 1)
        target = (row & 3) * 64 + (row >> 4) * 4 + ((row >> 2) & 3)
        perm[...] = (col == target).astype(F32).astype(BF16)

    def prepare_pick():
        small[2].wait()
        orders = order[...].astype(F32)
        for i in range(4):
            wide = jnp.broadcast_to(orders[i : i + 1], (128, 128))
            order_col[pl.ds(i * 128, 128)] = wide.T
        window = lax.broadcasted_iota(I32, (16, 512), 1).astype(F32)
        for g in range(GROUPS):
            for q in range(4):
                for h in range(2):
                    col = order_col[pl.ds(8 * g + 2 * q + h, 16, stride=SLOTS), :]
                    wide = jnp.concatenate([col] * 4, axis=1)
                    row = g * 128 + q * 32 + h * 16
                    pick[pl.ds(row, 16)] = (wide == window).astype(F32).astype(BF16)

    def root_event(g):
        if g == 0:
            root_copy.wait()

        def arrived(i, carry):
            source = lax.rem(me_o + i, N_ORDER)
            a2a_copy(g, source, source).wait_recv()
            return carry

        lax.fori_loop(1, N_ORDER, arrived, 0)

        row = lax.broadcasted_iota(I32, (32, 256), 0)
        col = lax.broadcasted_iota(I32, (32, 256), 1)
        keep = ((row >> 4) == ((col >> 6) & 1)) & ((row & 1) == (col >> 7))
        keep = keep.astype(F32).astype(BF16)
        first = (lax.broadcasted_iota(I32, (32, 128), 0) & 2) == 0

        def one(source, carry):
            r = recv_buf[g, source]
            r2 = jnp.concatenate([r, r], axis=1)
            lhs = jnp.concatenate([r2, r2], axis=0) * keep
            base = source * SLOTS + 8 * g
            wa = root[pl.ds(base, 4)].reshape(256, 128)
            wb = root[pl.ds(base + 4, 4)].reshape(256, 128)
            product = jnp.dot(
                lhs, jnp.concatenate([wa, wb], axis=1), preferred_element_type=F32
            )
            coef[pl.ds(pl.multiple_of(source * 32, 32), 32)] = jnp.where(
                first, product[:, :128], product[:, 128:]
            )
            return carry

        lax.fori_loop(0, N_ORDER, one, 0, unroll=4)
        for cc in range(4):
            parts = []
            for q in range(4):
                for h in range(2):
                    parts.append(coef[pl.ds(h * 16 + cc * 4 + q, 16, stride=32), :])
            coef_t[cc, :, pl.ds(g * 128, 128)] = jnp.concatenate(parts, axis=0).T.astype(BF16)

    def finish():
        degree = me_l * 128 + lax.broadcasted_iota(I32, (128, 512), 0)
        window = DEGREES // 512 * lax.broadcasted_iota(I32, (128, 512), 1)
        alive = degree >= window
        copies = []
        for cc in range(4):
            natural = jnp.dot(coef_t[cc], pick[...], preferred_element_type=F32)
            out[cc // 2, cc % 2] = jnp.where(alive, natural, 0.0).astype(BF16)
            copy = pltpu.make_async_copy(
                out.at[cc // 2, cc % 2], out_hbm.at[cc // 2, cc % 2], out_sem.at[cc]
            )
            copy.start()
            copies.append(copy)
        return copies

    small[0].wait()
    passed = False
    for event in schedule():
        if event[0] == "s" and event[1] == 0:
            c = event[2]
            start_event(c)
            if not passed:
                pl.semaphore_wait(barrier, LEVELS + N_ORDER - 1)
                small[1].wait()
                passed = True
            level_copy(0, c).start()
            all_loads[c][2].wait()
            own_terms(0, c)
        elif event[0] == "s":
            _, k, c = event
            level_event(k - 1, c)
            if k < LEVELS:
                level_copy(k, c).start()
                own_terms(k, c)
        elif event[0] == "a":
            a2a_event(event[1])
        elif event[0] == "p":
            prepare_perm()
            prepare_pick()
        else:
            root_event(event[1])
    out_copies = finish()
    for k in range(LEVELS):
        for c in range(CHUNKS):
            level_copy(k, c).wait_send()
    for g in range(GROUPS):

        def sent(i, carry):
            a2a_copy(g, lax.rem(me_o + i, N_ORDER), me_o).wait_send()
            return carry

        lax.fori_loop(1, N_ORDER, sent, 0)
    for copy in out_copies:
        copy.wait()


def per_device(
    fourier, quad_weights, leaf_basis, level_factors, sparsity, root_basis, order_of_slot
):
    anywhere = pl.BlockSpec(memory_space=pl.ANY)
    vmem = pltpu.VMEM
    return pl.pallas_call(
        kernel,
        out_shape=jax.ShapeDtypeStruct((2, 2, 128, 512), BF16),
        in_specs=[anywhere] * 7,
        out_specs=anywhere,
        scratch_shapes=[
            vmem((SLOTS, 64, 128), BF16),
            vmem((1, 128), F32),
            vmem((SLOTS, 64, 128), BF16),
            vmem((SLOTS, LEVELS, 2, 64, 64), BF16),
            pltpu.SMEM((LEVELS, 1, SLOTS), I32),
            vmem((512, 64, 128), BF16),
            vmem((4, 128), I32),
            vmem((2, 2, 128, 512), BF16),
            vmem((LEVELS + 1, CHUNKS, 2, RANK, 128), BF16),
            vmem((LEVELS, CHUNKS, 2, RANK, 128), BF16),
            vmem((LEVELS, CHUNKS, 2, RANK, 128), F32),
            vmem((256, 256), BF16),
            vmem((GROUPS, N_ORDER, 16, 128), BF16),
            vmem((GROUPS, N_ORDER, 16, 128), BF16),
            vmem((512, 128), F32),
            vmem((512, 512), BF16),
            vmem((512, 128), F32),
            vmem((4, 128, 512), BF16),
            pltpu.SemaphoreType.DMA((3, CHUNKS)),
            pltpu.SemaphoreType.DMA((3,)),
            pltpu.SemaphoreType.DMA,
            pltpu.SemaphoreType.DMA((4,)),
            pltpu.SemaphoreType.DMA((LEVELS, CHUNKS)),
            pltpu.SemaphoreType.DMA((LEVELS, CHUNKS)),
            pltpu.SemaphoreType.DMA((GROUPS, N_ORDER)),
            pltpu.SemaphoreType.DMA((GROUPS, N_ORDER)),
        ],
        compiler_params=pltpu.CompilerParams(
            collective_id=0, has_side_effects=True, vmem_limit_bytes=48 * 1024 * 1024
        ),
        cost_estimate=pl.CostEstimate(
            flops=2 * 10**9, bytes_accessed=15 * 10**6, transcendentals=0
        ),
    )(
        fourier,
        quad_weights.reshape(1, 128),
        leaf_basis,
        level_factors,
        sparsity.transpose(1, 2, 0),
        root_basis,
        order_of_slot.reshape(4, 128),
    )


def solution(mesh):
    return jax.shard_map(
        per_device,
        mesh=mesh,
        in_specs=(
            P("order", None, "lat"),
            P("lat"),
            P("order", None, "lat"),
            P("order", None, None, "lat", None, None),
            P("order", None, "lat"),
            P(None, None, "lat"),
            P(),
        ),
        out_specs=P("order", None, "lat", None),
        check_vma=False,
    )
```

time: 105 us -> 70.1 us (0.67)
  waiting for transfers between devices: 66.6 us -> 0 us
  Pallas kernels: 0 us -> 62.7 us
  starting transfers between devices: 19.2 us -> 0 us
  matrix products: 8.23 us -> 0 us
  other arithmetic: 2.42 us -> 0 us
    pallas_call x0 -> x1, Pallas kernels: none -> 62.7 us  [per_device(): pl.pallas_call(kernel, out_shape=jax.ShapeDtypeStruct((2, 2, 128, 512), B...]
    ppermute x4 -> x0, waiting for transfers between devices: 57.5 us -> none  [partner_2(): lax.ppermute(array, axis, [(i, i ^ 1 << bit) for i in range(lax.axis_size...]
    ppermute x4 -> x0, starting transfers between devices: 11.8 us -> none  [partner_2(): lax.ppermute(array, axis, [(i, i ^ 1 << bit) for i in range(lax.axis_size...]
    all_to_all x1 -> x0, waiting for transfers between devices: 9.03 us -> none  [per_device(): lax.all_to_all(coefficient, 'order', split_axis=2, concat_axis=0, tiled=T...]
    dot_general x9 -> x0, matrix products: 8.23 us -> none  [the longest x4 2.77 us: per_device(): jnp.einsum('ors,osc->orc', level_factors[:, depth_bit, 0, 0], rank_state,...]
    all_to_all x1 -> x0, starting transfers between devices: 7.39 us -> none  [per_device(): lax.all_to_all(coefficient, 'order', split_axis=2, concat_axis=0, tiled=T...]
    unnamed x4 -> x13, local copies, waits for them, and re-layouts: 1.05 us -> 7.08 us
    gather x2 -> x0, local copies, waits for them, and re-layouts: 2.83 us -> none  [per_device(): natural = jnp.take(arrived, inverse, axis=0)]
  transfers between devices with their start and end apart: 5 -> 0, of which waited for: 4 -> 0; matrix products, arithmetic and copies ran while one was open for 6% -> 0% of each run, Pallas kernels for 0% -> 0%
where the time goes in v1:
time: 70.1 us; the launch traced here: 69.8 us
  Pallas kernels  62.7 us (89%)
  local copies, waits for them, and re-layouts  7.08 us (10%)
    pallas_call x1, Pallas kernels, per_device(): pl.pallas_call(kernel, out_shape=jax.ShapeDtypeStruct((2, 2, 128, 512), B...  62.7 us
    unnamed x13, local copies, waits for them, and re-layouts  7.08 us

profile of v1, /device:TPU:8, one launch (start us, length us, event | category | flops | bytes accessed | tf_op | source)
XLA Modules:
  0.0 69.8 jit_solution(3903726884958944578)
XLA Ops:
  0.0 0.0 copy-start
  0.0 2.2 %copy-done = bf16[32,4,2,1,64,64]{5,4,3,2,1,0:T(8,128)(2,1)S(1)} copy-done((bf16[32,4,2,1,64,64]{5,4,3,2,1,0:T(8,128)(2,1)S(1)}, bf16[32,4,2,1,64,64]{5,4,3,2,1,0:T(8,128)(2,1)}, u32[]{:S(2)}) %copy-start) | copy-done | bytes 2097176
  2.2 0.0 copy-start.1
  2.2 1.0 %copy-done.1 = bf16[32,64,128]{2,1,0:T(8,128)(2,1)S(1)} copy-done((bf16[32,64,128]{2,1,0:T(8,128)(2,1)S(1)}, bf16[32,64,128]{2,1,0:T(8,128)(2,1)}, u32[]{:S(2)}) %copy-start.1) | copy-done | bytes 524312
  3.2 0.0 copy-start.2
  3.2 1.0 %copy-done.2 = bf16[32,64,128]{2,1,0:T(8,128)(2,1)S(1)} copy-done((bf16[32,64,128]{2,1,0:T(8,128)(2,1)S(1)}, bf16[32,64,128]{2,1,0:T(8,128)(2,1)}, u32[]{:S(2)}) %copy-start.2) | copy-done | bytes 524312
  4.3 0.0 copy-start.3
  4.3 0.7 copy-done.3
  5.0 0.0 copy-start.4
  5.0 0.7 copy-done.4
  5.6 0.0 copy-start.5
  5.6 0.7 copy-done.5
  6.3 62.7 %shard_map.73 = bf16[2,2,128,512]{3,2,1,0:T(8,128)(2,1)S(1)} custom-call(bf16[32,64,128]{2,1,0:T(8,128)(2,1)S(1)} %copy-done.1, f32[1,128]{1,0:T(1,128)S(1)} %bitcast.5, bf16[32,64,128]{2,1,0:T(8,128)(2,1)S(1)} %copy-done.2, bf16[32,4,2,1,64,64]{5,4,3,2,1,0:T(8,128)(2,1)S(1)} %copy-done, s32[4,1,32]{2,1,0:T(1,128)S(1)} %bitcast.3, ...), custom_call_target="tpu_custom_call" | custom-call | flops 2000000000 | bytes 15000000 | tf_op jit(solution)/shard_map/pallas_call | solution.py:283
  69.0 0.8 %copy.9 = bf16[2,2,128,512]{3,2,1,0:T(8,128)(2,1)} copy(bf16[2,2,128,512]{3,2,1,0:T(8,128)(2,1)S(1)} %shard_map.73) | data formatting | bytes 1048576
Async XLA Ops:
  0.0 2.2 %copy-start = (bf16[32,4,2,1,64,64]{5,4,3,2,1,0:T(8,128)(2,1)S(1)}, bf16[32,4,2,1,64,64]{5,4,3,2,1,0:T(8,128)(2,1)}, u32[]{:S(2)}) copy-start(bf16[32,4,2,1,64,64]{5,4,3,2,1,0:T(8,128)(2,1)} %fac_hbm.1) | copy-start | bytes 6291460
  2.2 1.0 %copy-start.1 = (bf16[32,64,128]{2,1,0:T(8,128)(2,1)S(1)}, bf16[32,64,128]{2,1,0:T(8,128)(2,1)}, u32[]{:S(2)}) copy-start(bf16[32,64,128]{2,1,0:T(8,128)(2,1)} %four_hbm.1) | copy-start | bytes 1572868
  3.2 1.0 %copy-start.2 = (bf16[32,64,128]{2,1,0:T(8,128)(2,1)S(1)}, bf16[32,64,128]{2,1,0:T(8,128)(2,1)}, u32[]{:S(2)}) copy-start(bf16[32,64,128]{2,1,0:T(8,128)(2,1)} %leaf_hbm.1) | copy-start | bytes 1572868
  4.3 0.7 copy-start.3
  5.0 0.7 copy-start.4
  5.6 0.7 copy-start.5

commit v2 on v1

--- a/solution.py
+++ b/solution.py
@@ -90,13 +90,26 @@
             device_id_type=MESH,
         )
 
-    def a2a_copy(g, dest, source):
+    shifted = [lax.rem(me_o + i, N_ORDER) for i in range(N_ORDER)]
+    others = pl.ds(1, N_ORDER - 1)
+
+    def a2a_copy(g, i):
         return pltpu.make_async_remote_copy(
-            src_ref=send_buf.at[g, dest],
-            dst_ref=recv_buf.at[g, source],
-            send_sem=a2a_send_sem.at[g, dest],
-            recv_sem=a2a_recv_sem.at[g, source],
-            device_id=(dest, me_l),
+            src_ref=send_buf.at[g, shifted[i]],
+            dst_ref=recv_buf.at[g, i],
+            send_sem=a2a_send_sem.at[g],
+            recv_sem=a2a_recv_sem.at[g],
+            device_id=(shifted[i], me_l),
+            device_id_type=MESH,
+        )
+
+    def a2a_all(g):
+        return pltpu.make_async_remote_copy(
+            src_ref=send_buf.at[g, others],
+            dst_ref=recv_buf.at[g, others],
+            send_sem=a2a_send_sem.at[g],
+            recv_sem=a2a_recv_sem.at[g],
+            device_id=(shifted[1], me_l),
             device_id_type=MESH,
         )
 
@@ -151,12 +164,9 @@
         ).astype(BF16)
         send_buf[g] = packed.reshape(N_ORDER, 16, 128)
 
-        def one(i, carry):
-            a2a_copy(g, lax.rem(me_o + i, N_ORDER), me_o).start()
-            return carry
-
-        lax.fori_loop(1, N_ORDER, one, 0)
-        recv_buf[g, me_o] = send_buf[g, me_o]
+        for i in range(1, N_ORDER):
+            a2a_copy(g, i).start()
+        recv_buf[g, 0] = send_buf[g, me_o]
 
     def prepare_perm():
         row = lax.broadcasted_iota(I32, (256, 256), 0)
@@ -183,12 +193,7 @@
         if g == 0:
             root_copy.wait()
 
-        def arrived(i, carry):
-            source = lax.rem(me_o + i, N_ORDER)
-            a2a_copy(g, source, source).wait_recv()
-            return carry
-
-        lax.fori_loop(1, N_ORDER, arrived, 0)
+        a2a_all(g).wait_recv()
 
         row = lax.broadcasted_iota(I32, (32, 256), 0)
         col = lax.broadcasted_iota(I32, (32, 256), 1)
@@ -196,8 +201,9 @@
         keep = keep.astype(F32).astype(BF16)
         first = (lax.broadcasted_iota(I32, (32, 128), 0) & 2) == 0
 
-        def one(source, carry):
-            r = recv_buf[g, source]
+        def one(i, carry):
+            source = lax.rem(me_o - i + N_ORDER, N_ORDER)
+            r = recv_buf[g, i]
             r2 = jnp.concatenate([r, r], axis=1)
             lhs = jnp.concatenate([r2, r2], axis=0) * keep
             base = source * SLOTS + 8 * g
@@ -265,12 +271,7 @@
         for c in range(CHUNKS):
             level_copy(k, c).wait_send()
     for g in range(GROUPS):
-
-        def sent(i, carry):
-            a2a_copy(g, lax.rem(me_o + i, N_ORDER), me_o).wait_send()
-            return carry
-
-        lax.fori_loop(1, N_ORDER, sent, 0)
+        a2a_all(g).wait_send()
     for copy in out_copies:
         copy.wait()
 
@@ -310,11 +311,11 @@
             pltpu.SemaphoreType.DMA((4,)),
             pltpu.SemaphoreType.DMA((LEVELS, CHUNKS)),
             pltpu.SemaphoreType.DMA((LEVELS, CHUNKS)),
-            pltpu.SemaphoreType.DMA((GROUPS, N_ORDER)),
-            pltpu.SemaphoreType.DMA((GROUPS, N_ORDER)),
+            pltpu.SemaphoreType.DMA((GROUPS,)),
+            pltpu.SemaphoreType.DMA((GROUPS,)),
         ],
         compiler_params=pltpu.CompilerParams(
-            collective_id=0, has_side_effects=True, vmem_limit_bytes=48 * 1024 * 1024
+            collective_id=0, has_side_effects=True, vmem_limit_bytes=60 * 1024 * 1024
         ),
         cost_estimate=pl.CostEstimate(
             flops=2 * 10**9, bytes_accessed=15 * 10**6, transcendentals=0

time: 70.1 us -> 61.2 us (0.87)
  local copies, waits for them, and re-layouts: 7.08 us -> 1.87 us
  Pallas kernels: 62.7 us -> 59.2 us
    unnamed x13 -> x1, local copies, waits for them, and re-layouts: 7.08 us -> 1.87 us
    pallas_call x1, Pallas kernels: 62.7 us -> 59.2 us  [per_device(): pl.pallas_call(kernel, out_shape=jax.ShapeDtypeStruct((2, 2, 128, 512), B...]
where the time goes in v2:
time: 61.2 us; the launch traced here: 61.1 us
  Pallas kernels  59.2 us (97%)
  local copies, waits for them, and re-layouts  1.87 us (3%)
    pallas_call x1, Pallas kernels, per_device(): pl.pallas_call(kernel, out_shape=jax.ShapeDtypeStruct((2, 2, 128, 512), B...  59.2 us
    unnamed x1, local copies, waits for them, and re-layouts  1.87 us

profile of v2, /device:TPU:8, one launch (start us, length us, event | category | flops | bytes accessed | tf_op | source)
XLA Modules:
  0.0 61.1 jit_solution(14055515354379173055)
XLA Ops:
  0.0 59.2 %shard_map.73 = bf16[2,2,128,512]{3,2,1,0:T(8,128)(2,1)} custom-call(bf16[32,64,128]{2,1,0:T(8,128)(2,1)} %four_hbm.1, f32[1,128]{1,0:T(1,128)} %bitcast.5, bf16[32,64,128]{2,1,0:T(8,128)(2,1)} %leaf_hbm.1, bf16[32,4,2,1,64,64]{5,4,3,2,1,0:T(8,128)(2,1)} %fac_hbm.1, s32[4,1,32]{2,1,0:T(1,128)} %bitcast.3, bf16[512,64,128]{2,1,0:T(8,128)(2,1)} %root_hbm.1, ...), custom_call_target="tpu_custom_call" | custom-call | flops 2000000000 | bytes 15000000 | tf_op jit(solution)/shard_map/pallas_call | solution.py:284
  59.2 1.9 %copy.9 = bf16[2,2,128,512]{3,2,1,0:T(8,128)(2,1)} copy(bf16[2,2,128,512]{3,2,1,0:T(8,128)(2,1)} %shard_map.73) | data formatting | bytes 1048576

commit v3 on v2

--- a/solution.py
+++ b/solution.py
@@ -23,7 +23,7 @@
 
 
 def schedule():
-    events = []
+
     keyed = []
     for c in range(CHUNKS):
         keyed.append((c * 1.0, 0, ("s", 0, c)))
@@ -32,12 +32,10 @@
         keyed.append((c * 2.0 + 12.0, 3, ("s", 3, c)))
         keyed.append((c * 2.0 + 18.5, 4, ("s", 4, c)))
     for g in range(GROUPS):
-        keyed.append(((2 * g + 1) * 2.0 + 18.6, 5, ("a", g)))
-        keyed.append(((2 * g + 1) * 2.0 + 18.6 + 3.5, 6, ("r", g)))
+        keyed.append(((2 * g + 1) * 2.0 + 18.5 + 0.1, 5, ("a", g)))
+        keyed.append((99 + g, 6, ("r", g)))
     keyed.append((8.1, 7, ("p",)))
-    for _, _, event in sorted(keyed):
-        events.append(event)
-    return events
+    return [e for _, _, e in sorted(keyed)]
 
 
 def kernel(

time: 61.2 us -> 50.5 us (0.83)
  Pallas kernels: 59.2 us -> 48.4 us
    pallas_call x1, Pallas kernels: 59.2 us -> 48.4 us  [per_device(): pl.pallas_call(kernel, out_shape=jax.ShapeDtypeStruct((2, 2, 128, 512), B...]
where the time goes in v3:
time: 50.5 us; the launch traced here: 50.3 us
  Pallas kernels  48.4 us (96%)
  local copies, waits for them, and re-layouts  1.87 us (4%)
    pallas_call x1, Pallas kernels, per_device(): pl.pallas_call(kernel, out_shape=jax.ShapeDtypeStruct((2, 2, 128, 512), B...  48.4 us
    unnamed x1, local copies, waits for them, and re-layouts  1.87 us

profile of v3, /device:TPU:8, one launch (start us, length us, event | category | flops | bytes accessed | tf_op | source)
XLA Modules:
  0.0 50.3 jit_solution(4548202564896726765)
XLA Ops:
  0.0 48.4 %shard_map.73 = bf16[2,2,128,512]{3,2,1,0:T(8,128)(2,1)} custom-call(bf16[32,64,128]{2,1,0:T(8,128)(2,1)} %four_hbm.1, f32[1,128]{1,0:T(1,128)} %bitcast.5, bf16[32,64,128]{2,1,0:T(8,128)(2,1)} %leaf_hbm.1, bf16[32,4,2,1,64,64]{5,4,3,2,1,0:T(8,128)(2,1)} %fac_hbm.1, s32[4,1,32]{2,1,0:T(1,128)} %bitcast.3, bf16[512,64,128]{2,1,0:T(8,128)(2,1)} %root_hbm.1, ...), custom_call_target="tpu_custom_call" | custom-call | flops 2000000000 | bytes 15000000 | tf_op jit(solution)/shard_map/pallas_call | solution.py:282
  48.4 1.9 %copy.9 = bf16[2,2,128,512]{3,2,1,0:T(8,128)(2,1)} copy(bf16[2,2,128,512]{3,2,1,0:T(8,128)(2,1)} %shard_map.73) | data formatting | bytes 1048576

commit v4 on v3

--- a/solution.py
+++ b/solution.py
@@ -17,30 +17,35 @@
 CHUNK = 4
 CHUNKS = SLOTS // CHUNK
 LEVELS = 4
-GROUPS = 4
+GROUPS = ((0, 1), (2, 3), (4, 5), (6,), (7,))
+LAST = len(GROUPS) - 1
 N_ORDER = 16
 RANK = 64
 
 
+HOPS = [(0, 1, 2, 1)[k >> 2] + (0, 1, 2, 1)[k & 3] for k in range(N_ORDER)]
+NEAR = [k for k in range(1, N_ORDER) if HOPS[k] <= 2]
+FAR = [k for k in range(1, N_ORDER) if HOPS[k] > 2]
+
+
 def schedule():
-
     keyed = []
     for c in range(CHUNKS):
         keyed.append((c * 1.0, 0, ("s", 0, c)))
         keyed.append((c * 1.0 + 2.5, 1, ("s", 1, c)))
-        keyed.append((c * 1.0 + 5.5, 2, ("s", 2, c)))
-        keyed.append((c * 2.0 + 12.0, 3, ("s", 3, c)))
-        keyed.append((c * 2.0 + 18.5, 4, ("s", 4, c)))
-    for g in range(GROUPS):
-        keyed.append(((2 * g + 1) * 2.0 + 18.5 + 0.1, 5, ("a", g)))
-        keyed.append((99 + g, 6, ("r", g)))
+        keyed.append((c * 2.0 + 5.5, 2, ("s", 2, c)))
+        keyed.append((c * 2.0 + 13.6, 3, ("s", 3, c)))
+        keyed.append((c * 2.0 + 21.7, 4, ("s", 4, c)))
+    for g, chunks in enumerate(GROUPS):
+        keyed.append((chunks[-1] * 2.0 + 21.8, 5, ("a", g)))
+        keyed.append((999 + g, 6, ("r", g)))
     keyed.append((8.1, 7, ("p",)))
-    return [e for _, _, e in sorted(keyed)]
+    return [event for _, _, event in sorted(keyed)]
 
 
 def kernel(
-    four_hbm, quad_hbm, leaf_hbm, fac_hbm, spars_hbm, root_hbm, order_hbm, out_hbm,
-    four, quad, leaf, fac, spars, root, order, out,
+    four_hbm, quad_hbm, leaf_hbm, fac_hbm, spars_hbm, root_hbm, order_hbm, coef_hbm, pick_hbm,
+    four, quad, leaf, fac, spars, root, order,
     state, partner, own, perm, send_buf, recv_buf, order_col, pick, coef, coef_t,
     in_sem, small_sem, root_sem, out_sem, send_sem, recv_sem, a2a_send_sem, a2a_recv_sem,
 ):
@@ -88,26 +93,23 @@
             device_id_type=MESH,
         )
 
-    shifted = [lax.rem(me_o + i, N_ORDER) for i in range(N_ORDER)]
-    others = pl.ds(1, N_ORDER - 1)
-
-    def a2a_copy(g, i):
+    def a2a_copy(g, k):
         return pltpu.make_async_remote_copy(
-            src_ref=send_buf.at[g, shifted[i]],
-            dst_ref=recv_buf.at[g, i],
+            src_ref=send_buf.at[g, me_o ^ k],
+            dst_ref=recv_buf.at[g, k],
             send_sem=a2a_send_sem.at[g],
-            recv_sem=a2a_recv_sem.at[g],
-            device_id=(shifted[i], me_l),
+            recv_sem=a2a_recv_sem.at[g, int(g == LAST and k in FAR)],
+            device_id=(me_o ^ k, me_l),
             device_id_type=MESH,
         )
 
-    def a2a_all(g):
+    def a2a_bytes(g, count, far=0):
         return pltpu.make_async_remote_copy(
-            src_ref=send_buf.at[g, others],
-            dst_ref=recv_buf.at[g, others],
+            src_ref=send_buf.at[g, pl.ds(0, count)],
+            dst_ref=recv_buf.at[g, pl.ds(0, count)],
             send_sem=a2a_send_sem.at[g],
-            recv_sem=a2a_recv_sem.at[g],
-            device_id=(shifted[1], me_l),
+            recv_sem=a2a_recv_sem.at[g, far],
+            device_id=(me_o ^ 1, me_l),
             device_id_type=MESH,
         )
 
@@ -150,20 +152,16 @@
             state[k + 1, c, h] = (own[k, c, h] + present * cross).astype(BF16)
 
     def a2a_event(g):
-        x = jnp.concatenate(
-            [
-                state[LEVELS, 2 * g].reshape(2 * RANK, 128),
-                state[LEVELS, 2 * g + 1].reshape(2 * RANK, 128),
-            ],
-            axis=1,
-        )
+        x = [state[LEVELS, c].reshape(2 * RANK, 128) for c in GROUPS[g]]
         packed = lax.dot_general(
-            perm[...], x, (((1,), (1,)), ((), ())), preferred_element_type=F32
+            perm[:, : 128 * len(x)],
+            jnp.concatenate(x, axis=1),
+            (((1,), (1,)), ((), ())),
+            preferred_element_type=F32,
         ).astype(BF16)
         send_buf[g] = packed.reshape(N_ORDER, 16, 128)
-
-        for i in range(1, N_ORDER):
-            a2a_copy(g, i).start()
+        for k in sorted(NEAR + FAR, key=lambda k: -HOPS[k]):
+            a2a_copy(g, k).start()
         recv_buf[g, 0] = send_buf[g, me_o]
 
     def prepare_perm():
@@ -179,64 +177,73 @@
             wide = jnp.broadcast_to(orders[i : i + 1], (128, 128))
             order_col[pl.ds(i * 128, 128)] = wide.T
         window = lax.broadcasted_iota(I32, (16, 512), 1).astype(F32)
-        for g in range(GROUPS):
+        for g in range(SLOTS // 8):
             for q in range(4):
                 for h in range(2):
                     col = order_col[pl.ds(8 * g + 2 * q + h, 16, stride=SLOTS), :]
                     wide = jnp.concatenate([col] * 4, axis=1)
                     row = g * 128 + q * 32 + h * 16
                     pick[pl.ds(row, 16)] = (wide == window).astype(F32).astype(BF16)
+        pick_copy.start()
 
     def root_event(g):
         if g == 0:
             root_copy.wait()
-
-        a2a_all(g).wait_recv()
-
+        pair = len(GROUPS[g]) == 2
         row = lax.broadcasted_iota(I32, (32, 256), 0)
         col = lax.broadcasted_iota(I32, (32, 256), 1)
         keep = ((row >> 4) == ((col >> 6) & 1)) & ((row & 1) == (col >> 7))
         keep = keep.astype(F32).astype(BF16)
         first = (lax.broadcasted_iota(I32, (32, 128), 0) & 2) == 0
 
-        def one(i, carry):
-            source = lax.rem(me_o - i + N_ORDER, N_ORDER)
-            r = recv_buf[g, i]
+        def one(k):
+            source = me_o ^ k
+            r = recv_buf[g, k]
             r2 = jnp.concatenate([r, r], axis=1)
             lhs = jnp.concatenate([r2, r2], axis=0) * keep
-            base = source * SLOTS + 8 * g
-            wa = root[pl.ds(base, 4)].reshape(256, 128)
-            wb = root[pl.ds(base + 4, 4)].reshape(256, 128)
-            product = jnp.dot(
-                lhs, jnp.concatenate([wa, wb], axis=1), preferred_element_type=F32
-            )
-            coef[pl.ds(pl.multiple_of(source * 32, 32), 32)] = jnp.where(
-                first, product[:, :128], product[:, 128:]
-            )
-            return carry
-
-        lax.fori_loop(0, N_ORDER, one, 0, unroll=4)
+            base = source * SLOTS + GROUPS[g][0] * CHUNK
+            w = root[pl.ds(base, 4)].reshape(256, 128)
+            if pair:
+                w = jnp.concatenate([w, root[pl.ds(base + 4, 4)].reshape(256, 128)], axis=1)
+            product = jnp.dot(lhs, w, preferred_element_type=F32)
+            if pair:
+                product = jnp.where(first, product[:, :128], product[:, 128:])
+            coef[pl.ds(pl.multiple_of(source * 32, 32), 32)] = product
+
+        if g == LAST:
+            one(0)
+            a2a_bytes(g, len(NEAR), 0).wait_recv()
+            for k in NEAR:
+                one(k)
+            a2a_bytes(g, len(FAR), 1).wait_recv()
+            for k in FAR:
+                one(k)
+        else:
+            a2a_bytes(g, N_ORDER - 1).wait_recv()
+
+            def body(k, carry):
+                one(k)
+                return carry
+
+            lax.fori_loop(0, N_ORDER, body, 0, unroll=4)
+        width = 128 if pair else 64
+        lanes = pl.ds(GROUPS[g][0] * 64, width)
         for cc in range(4):
             parts = []
-            for q in range(4):
+            for q in range(width // 32):
                 for h in range(2):
                     parts.append(coef[pl.ds(h * 16 + cc * 4 + q, 16, stride=32), :])
-            coef_t[cc, :, pl.ds(g * 128, 128)] = jnp.concatenate(parts, axis=0).T.astype(BF16)
-
-    def finish():
-        degree = me_l * 128 + lax.broadcasted_iota(I32, (128, 512), 0)
-        window = DEGREES // 512 * lax.broadcasted_iota(I32, (128, 512), 1)
-        alive = degree >= window
-        copies = []
-        for cc in range(4):
-            natural = jnp.dot(coef_t[cc], pick[...], preferred_element_type=F32)
-            out[cc // 2, cc % 2] = jnp.where(alive, natural, 0.0).astype(BF16)
-            copy = pltpu.make_async_copy(
-                out.at[cc // 2, cc % 2], out_hbm.at[cc // 2, cc % 2], out_sem.at[cc]
-            )
-            copy.start()
-            copies.append(copy)
-        return copies
+            coef_t[cc, :, lanes] = jnp.concatenate(parts, axis=0).T.astype(BF16)
+        if pair or g == LAST:
+            coef_copy(g if pair else 3).start()
+
+    def coef_copy(block):
+        lanes = pl.ds(block * 128, 128)
+        return pltpu.make_async_copy(
+            coef_t.at[:, :, lanes], coef_hbm.at[:, :, lanes], out_sem.at[block]
+        )
+
+    pick_copy = pltpu.make_async_copy(pick, pick_hbm, out_sem.at[4])
 
     small[0].wait()
     passed = False
@@ -264,12 +271,36 @@
             prepare_pick()
         else:
             root_event(event[1])
-    out_copies = finish()
     for k in range(LEVELS):
         for c in range(CHUNKS):
             level_copy(k, c).wait_send()
-    for g in range(GROUPS):
-        a2a_all(g).wait_send()
+    for g in range(len(GROUPS)):
+        a2a_bytes(g, N_ORDER - 1).wait_send()
+    pick_copy.wait()
+    for block in range(4):
+        coef_copy(block).wait()
+
+
+def finish_kernel(coef_hbm, pick_hbm, out_hbm, coef_t, pick, out, in_sem, out_sem):
+    pick_copy = pltpu.make_async_copy(pick_hbm, pick, in_sem.at[4])
+    coef_copies = [
+        pltpu.make_async_copy(coef_hbm.at[cc], coef_t.at[cc], in_sem.at[cc]) for cc in range(4)
+    ]
+    pick_copy.start()
+    for copy in coef_copies:
+        copy.start()
+    degree = lax.axis_index("lat") * 128 + lax.broadcasted_iota(I32, (128, 512), 0)
+    window = DEGREES // 512 * lax.broadcasted_iota(I32, (128, 512), 1)
+    alive = degree >= window
+    pick_copy.wait()
+    out_copies = []
+    for cc in range(4):
+        coef_copies[cc].wait()
+        natural = jnp.dot(coef_t[cc], pick[...], preferred_element_type=F32)
+        out[cc] = jnp.where(alive, natural, 0.0).astype(BF16)
+        copy = pltpu.make_async_copy(out.at[cc], out_hbm.at[cc // 2, cc % 2], out_sem.at[cc])
+        copy.start()
+        out_copies.append(copy)
     for copy in out_copies:
         copy.wait()
 
@@ -279,11 +310,14 @@
 ):
     anywhere = pl.BlockSpec(memory_space=pl.ANY)
     vmem = pltpu.VMEM
-    return pl.pallas_call(
+    coef, pick = pl.pallas_call(
         kernel,
-        out_shape=jax.ShapeDtypeStruct((2, 2, 128, 512), BF16),
+        out_shape=[
+            jax.ShapeDtypeStruct((4, 128, 512), BF16),
+            jax.ShapeDtypeStruct((512, 512), BF16),
+        ],
         in_specs=[anywhere] * 7,
-        out_specs=anywhere,
+        out_specs=[anywhere] * 2,
         scratch_shapes=[
             vmem((SLOTS, 64, 128), BF16),
             vmem((1, 128), F32),
@@ -292,13 +326,12 @@
             pltpu.SMEM((LEVELS, 1, SLOTS), I32),
             vmem((512, 64, 128), BF16),
             vmem((4, 128), I32),
-            vmem((2, 2, 128, 512), BF16),
             vmem((LEVELS + 1, CHUNKS, 2, RANK, 128), BF16),
             vmem((LEVELS, CHUNKS, 2, RANK, 128), BF16),
             vmem((LEVELS, CHUNKS, 2, RANK, 128), F32),
             vmem((256, 256), BF16),
-            vmem((GROUPS, N_ORDER, 16, 128), BF16),
-            vmem((GROUPS, N_ORDER, 16, 128), BF16),
+            vmem((len(GROUPS), N_ORDER, 16, 128), BF16),
+            vmem((len(GROUPS), N_ORDER, 16, 128), BF16),
             vmem((512, 128), F32),
             vmem((512, 512), BF16),
             vmem((512, 128), F32),
@@ -306,11 +339,11 @@
             pltpu.SemaphoreType.DMA((3, CHUNKS)),
             pltpu.SemaphoreType.DMA((3,)),
             pltpu.SemaphoreType.DMA,
-            pltpu.SemaphoreType.DMA((4,)),
+            pltpu.SemaphoreType.DMA((5,)),
             pltpu.SemaphoreType.DMA((LEVELS, CHUNKS)),
             pltpu.SemaphoreType.DMA((LEVELS, CHUNKS)),
-            pltpu.SemaphoreType.DMA((GROUPS,)),
-            pltpu.SemaphoreType.DMA((GROUPS,)),
+            pltpu.SemaphoreType.DMA((len(GROUPS),)),
+            pltpu.SemaphoreType.DMA((len(GROUPS), 2)),
         ],
         compiler_params=pltpu.CompilerParams(
             collective_id=0, has_side_effects=True, vmem_limit_bytes=60 * 1024 * 1024
@@ -327,6 +360,23 @@
         root_basis,
         order_of_slot.reshape(4, 128),
     )
+    return pl.pallas_call(
+        finish_kernel,
+        out_shape=jax.ShapeDtypeStruct((2, 2, 128, 512), BF16),
+        in_specs=[anywhere] * 2,
+        out_specs=anywhere,
+        scratch_shapes=[
+            vmem((4, 128, 512), BF16),
+            vmem((512, 512), BF16),
+            vmem((4, 128, 512), BF16),
+            pltpu.SemaphoreType.DMA((5,)),
+            pltpu.SemaphoreType.DMA((4,)),
+        ],
+        compiler_params=pltpu.CompilerParams(vmem_limit_bytes=60 * 1024 * 1024),
+        cost_estimate=pl.CostEstimate(
+            flops=2 * 512**3, bytes_accessed=3 * 2**19, transcendentals=0
+        ),
+    )(coef, pick)
 
 
 def solution(mesh):

time: 50.5 us -> 51 us (level)
  Pallas kernels: 48.4 us -> 50.3 us
  local copies, waits for them, and re-layouts: 1.87 us -> 0 us
    unnamed x1 -> x0, local copies, waits for them, and re-layouts: 1.87 us -> none
    pallas_call x1 -> x2, Pallas kernels: 48.4 us -> 50.3 us  [the longest x1 47.5 us: per_device(): pl.pallas_call(kernel, out_shape=[jax.ShapeDtypeStruct((4, 128, 512), BF1...]
where the time goes in v4:
time: 51 us; the launch traced here: 50.3 us
  Pallas kernels  50.3 us (99%)
    pallas_call x1, Pallas kernels, per_device(): pl.pallas_call(kernel, out_shape=[jax.ShapeDtypeStruct((4, 128, 512), BF1...  47.5 us
    pallas_call x1, Pallas kernels, per_device(): pl.pallas_call(finish_kernel, out_shape=jax.ShapeDtypeStruct((2, 2, 128,...  2.74 us

profile of v4, /device:TPU:8, one launch (start us, length us, event | category | flops | bytes accessed | tf_op | source)
XLA Modules:
  0.0 50.3 jit_solution(4560543534750251645)
XLA Ops:
  0.0 47.5 %shard_map.73 = (bf16[4,128,512]{2,1,0:T(8,128)(2,1)}, bf16[512,512]{1,0:T(8,128)(2,1)}) custom-call(bf16[32,64,128]{2,1,0:T(8,128)(2,1)} %four_hbm.1, f32[1,128]{1,0:T(1,128)} %bitcast.5, bf16[32,64,128]{2,1,0:T(8,128)(2,1)} %leaf_hbm.1, bf16[32,4,2,1,64,64]{5,4,3,2,1,0:T(8,128)(2,1)} %fac_hbm.1, s32[4,1,32]{2,1,0:T(1,128)} %bitcast.3, ...), custom_call_target="tpu_custom_call" | custom-call | flops 2000000000 | bytes 15000000 | tf_op jit(solution)/shard_map/pallas_call | solution.py:313
  47.6 2.7 %shard_map.74 = bf16[2,2,128,512]{3,2,1,0:T(8,128)(2,1)} custom-call(bf16[4,128,512]{2,1,0:T(8,128)(2,1)} %get-tuple-element.7.coef_hbm, bf16[512,512]{1,0:T(8,128)(2,1)} %get-tuple-element.8.pick_hbm), custom_call_target="tpu_custom_call" | custom-call | flops 268435456 | bytes 1572864 | tf_op jit(solution)/shard_map/pallas_call | solution.py:363

commit v5 on v4

--- a/solution.py
+++ b/solution.py
@@ -33,20 +33,20 @@
     for c in range(CHUNKS):
         keyed.append((c * 1.0, 0, ("s", 0, c)))
         keyed.append((c * 1.0 + 2.5, 1, ("s", 1, c)))
-        keyed.append((c * 2.0 + 5.5, 2, ("s", 2, c)))
-        keyed.append((c * 2.0 + 13.6, 3, ("s", 3, c)))
-        keyed.append((c * 2.0 + 21.7, 4, ("s", 4, c)))
+        keyed.append((c * 1.0 + 5.5, 2, ("s", 2, c)))
+        keyed.append((c * 2.0 + 12.0, 3, ("s", 3, c)))
+        keyed.append((c * 2.0 + 18.5, 4, ("s", 4, c)))
     for g, chunks in enumerate(GROUPS):
-        keyed.append((chunks[-1] * 2.0 + 21.8, 5, ("a", g)))
+        keyed.append((chunks[-1] * 2.0 + 18.6, 5, ("a", g)))
         keyed.append((999 + g, 6, ("r", g)))
     keyed.append((8.1, 7, ("p",)))
     return [event for _, _, event in sorted(keyed)]
 
 
 def kernel(
-    four_hbm, quad_hbm, leaf_hbm, fac_hbm, spars_hbm, root_hbm, order_hbm, coef_hbm, pick_hbm,
+    four_hbm, quad_hbm, leaf_hbm, fac_hbm, spars_hbm, root_hbm, order_hbm, part_hbm, coef_hbm, pick_hbm,
     four, quad, leaf, fac, spars, root, order,
-    state, partner, own, perm, send_buf, recv_buf, order_col, pick, coef, coef_t,
+    state, partner, own, perm, send_buf, recv_buf, order_col, pick, coef, coef_t, part,
     in_sem, small_sem, root_sem, out_sem, send_sem, recv_sem, a2a_send_sem, a2a_recv_sem,
 ):
     me_o = lax.axis_index("order")
@@ -68,12 +68,8 @@
     ]
     root_copy = pltpu.make_async_copy(root_hbm, root, root_sem)
     all_loads = [loads(c) for c in range(CHUNKS)]
-    for copy in small:
+    for copy in (all_loads[0][0], all_loads[0][1], small[0]):
         copy.start()
-    for c in range(CHUNKS):
-        for copy in all_loads[c]:
-            copy.start()
-    root_copy.start()
 
     barrier = pltpu.get_barrier_semaphore()
     for peer in peers:
@@ -82,6 +78,14 @@
         pl.semaphore_signal(
             barrier, inc=1, device_id=(lax.rem(me_o + i, N_ORDER), me_l), device_id_type=MESH
         )
+
+    for c in range(1, CHUNKS):
+        for copy in all_loads[c][:2]:
+            copy.start()
+    for copy in small[1:]:
+        copy.start()
+    for c in range(CHUNKS):
+        all_loads[c][2].start()
 
     def level_copy(k, c):
         return pltpu.make_async_remote_copy(
@@ -234,16 +238,17 @@
                 for h in range(2):
                     parts.append(coef[pl.ds(h * 16 + cc * 4 + q, 16, stride=32), :])
             coef_t[cc, :, lanes] = jnp.concatenate(parts, axis=0).T.astype(BF16)
-        if pair or g == LAST:
-            coef_copy(g if pair else 3).start()
-
-    def coef_copy(block):
-        lanes = pl.ds(block * 128, 128)
-        return pltpu.make_async_copy(
-            coef_t.at[:, :, lanes], coef_hbm.at[:, :, lanes], out_sem.at[block]
-        )
-
-    pick_copy = pltpu.make_async_copy(pick, pick_hbm, out_sem.at[4])
+        if g == 2:
+            part[...] = jnp.dot(
+                coef_t[:, :, :384].reshape(512, 384), pick[:384], preferred_element_type=F32
+            ).astype(BF16)
+            part_copy.start()
+        if g == LAST:
+            coef_copy.start()
+
+    coef_copy = pltpu.make_async_copy(coef_t.at[:, :, pl.ds(384, 128)], coef_hbm, out_sem.at[0])
+    pick_copy = pltpu.make_async_copy(pick.at[pl.ds(384, 128)], pick_hbm, out_sem.at[1])
+    part_copy = pltpu.make_async_copy(part, part_hbm, out_sem.at[2])
 
     small[0].wait()
     passed = False
@@ -253,13 +258,15 @@
             start_event(c)
             if not passed:
                 pl.semaphore_wait(barrier, LEVELS + N_ORDER - 1)
-                small[1].wait()
                 passed = True
             level_copy(0, c).start()
-            all_loads[c][2].wait()
-            own_terms(0, c)
         elif event[0] == "s":
             _, k, c = event
+            if event == ("s", 1, 0):
+                small[1].wait()
+            if k == 1:
+                all_loads[c][2].wait()
+                own_terms(0, c)
             level_event(k - 1, c)
             if k < LEVELS:
                 level_copy(k, c).start()
@@ -267,6 +274,7 @@
         elif event[0] == "a":
             a2a_event(event[1])
         elif event[0] == "p":
+            root_copy.start()
             prepare_perm()
             prepare_pick()
         else:
@@ -276,28 +284,29 @@
             level_copy(k, c).wait_send()
     for g in range(len(GROUPS)):
         a2a_bytes(g, N_ORDER - 1).wait_send()
-    pick_copy.wait()
-    for block in range(4):
-        coef_copy(block).wait()
-
-
-def finish_kernel(coef_hbm, pick_hbm, out_hbm, coef_t, pick, out, in_sem, out_sem):
-    pick_copy = pltpu.make_async_copy(pick_hbm, pick, in_sem.at[4])
-    coef_copies = [
-        pltpu.make_async_copy(coef_hbm.at[cc], coef_t.at[cc], in_sem.at[cc]) for cc in range(4)
+    for copy in (pick_copy, part_copy, coef_copy):
+        copy.wait()
+
+
+def finish_kernel(part_hbm, coef_hbm, pick_hbm, out_hbm, part, coef_t, pick, out, in_sem, out_sem):
+    copies = [
+        pltpu.make_async_copy(coef_hbm, coef_t, in_sem.at[0]),
+        pltpu.make_async_copy(pick_hbm, pick, in_sem.at[1]),
+        pltpu.make_async_copy(part_hbm, part, in_sem.at[2]),
     ]
-    pick_copy.start()
-    for copy in coef_copies:
+    for copy in copies:
         copy.start()
     degree = lax.axis_index("lat") * 128 + lax.broadcasted_iota(I32, (128, 512), 0)
     window = DEGREES // 512 * lax.broadcasted_iota(I32, (128, 512), 1)
     alive = degree >= window
-    pick_copy.wait()
+    for copy in copies:
+        copy.wait()
+    natural = jnp.dot(coef_t[...].reshape(512, 128), pick[...], preferred_element_type=F32)
     out_copies = []
     for cc in range(4):
-        coef_copies[cc].wait()
-        natural = jnp.dot(coef_t[cc], pick[...], preferred_element_type=F32)
-        out[cc] = jnp.where(alive, natural, 0.0).astype(BF16)
+        rows = slice(cc * 128, (cc + 1) * 128)
+        total = part[rows].astype(F32) + natural[rows]
+        out[cc] = jnp.where(alive, total, 0.0).astype(BF16)
         copy = pltpu.make_async_copy(out.at[cc], out_hbm.at[cc // 2, cc % 2], out_sem.at[cc])
         copy.start()
         out_copies.append(copy)
@@ -310,14 +319,15 @@
 ):
     anywhere = pl.BlockSpec(memory_space=pl.ANY)
     vmem = pltpu.VMEM
-    coef, pick = pl.pallas_call(
+    parts = pl.pallas_call(
         kernel,
         out_shape=[
-            jax.ShapeDtypeStruct((4, 128, 512), BF16),
             jax.ShapeDtypeStruct((512, 512), BF16),
+            jax.ShapeDtypeStruct((4, 128, 128), BF16),
+            jax.ShapeDtypeStruct((128, 512), BF16),
         ],
         in_specs=[anywhere] * 7,
-        out_specs=[anywhere] * 2,
+        out_specs=[anywhere] * 3,
         scratch_shapes=[
             vmem((SLOTS, 64, 128), BF16),
             vmem((1, 128), F32),
@@ -336,10 +346,11 @@
             vmem((512, 512), BF16),
             vmem((512, 128), F32),
             vmem((4, 128, 512), BF16),
+            vmem((512, 512), BF16),
             pltpu.SemaphoreType.DMA((3, CHUNKS)),
             pltpu.SemaphoreType.DMA((3,)),
             pltpu.SemaphoreType.DMA,
-            pltpu.SemaphoreType.DMA((5,)),
+            pltpu.SemaphoreType.DMA((3,)),
             pltpu.SemaphoreType.DMA((LEVELS, CHUNKS)),
             pltpu.SemaphoreType.DMA((LEVELS, CHUNKS)),
             pltpu.SemaphoreType.DMA((len(GROUPS),)),
@@ -363,20 +374,21 @@
     return pl.pallas_call(
         finish_kernel,
         out_shape=jax.ShapeDtypeStruct((2, 2, 128, 512), BF16),
-        in_specs=[anywhere] * 2,
+        in_specs=[anywhere] * 3,
         out_specs=anywhere,
         scratch_shapes=[
+            vmem((512, 512), BF16),
+            vmem((4, 128, 128), BF16),
+            vmem((128, 512), BF16),
             vmem((4, 128, 512), BF16),
-            vmem((512, 512), BF16),
-            vmem((4, 128, 512), BF16),
-            pltpu.SemaphoreType.DMA((5,)),
+            pltpu.SemaphoreType.DMA((3,)),
             pltpu.SemaphoreType.DMA((4,)),
         ],
         compiler_params=pltpu.CompilerParams(vmem_limit_bytes=60 * 1024 * 1024),
         cost_estimate=pl.CostEstimate(
-            flops=2 * 512**3, bytes_accessed=3 * 2**19, transcendentals=0
+            flops=2**26, bytes_accessed=5 * 2**18, transcendentals=0
         ),
-    )(coef, pick)
+    )(*parts)
 
 
 def solution(mesh):

time: 51 us -> 50.1 us (0.982)
  Pallas kernels: 50.3 us -> 49.7 us
    pallas_call x1, Pallas kernels: 2.74 us -> 2.2 us  [per_device(): pl.pallas_call(finish_kernel, out_shape=jax.ShapeDtypeStruct((2, 2, 128,...]
where the time goes in v5:
time: 50.1 us; the launch traced here: 49.7 us
  Pallas kernels  49.7 us (99%)
    pallas_call x1, Pallas kernels, per_device(): pl.pallas_call(kernel, out_shape=[jax.ShapeDtypeStruct((512, 512), BF16),...  47.5 us
    pallas_call x1, Pallas kernels, per_device(): pl.pallas_call(finish_kernel, out_shape=jax.ShapeDtypeStruct((2, 2, 128,...  2.2 us

profile of v5, /device:TPU:8, one launch (start us, length us, event | category | flops | bytes accessed | tf_op | source)
XLA Modules:
  0.0 49.7 jit_solution(6737514944368465921)
XLA Ops:
  0.0 47.5 %shard_map.73 = (bf16[512,512]{1,0:T(8,128)(2,1)}, bf16[4,128,128]{2,1,0:T(8,128)(2,1)}, bf16[128,512]{1,0:T(8,128)(2,1)}) custom-call(bf16[32,64,128]{2,1,0:T(8,128)(2,1)} %four_hbm.1, f32[1,128]{1,0:T(1,128)} %bitcast.5, bf16[32,64,128]{2,1,0:T(8,128)(2,1)} %leaf_hbm.1, bf16[32,4,2,1,64,64]{5,4,3,2,1,0:T(8,128)(2,1)} %fac_hbm.1, s32[4,1,32]{2,1,0:T(1,128)} %bitcast.3, ...), custom_call_target="tpu_custom_call" | custom-call | flops 2000000000 | bytes 15000000 | tf_op jit(solution)/shard_map/pallas_call | solution.py:322
  47.5 2.2 %shard_map.74 = bf16[2,2,128,512]{3,2,1,0:T(8,128)(2,1)} custom-call(bf16[512,512]{1,0:T(8,128)(2,1)} %get-tuple-element.8.part_hbm, bf16[4,128,128]{2,1,0:T(8,128)(2,1)} %get-tuple-element.9.coef_hbm, bf16[128,512]{1,0:T(8,128)(2,1)} %get-tuple-element.10.pick_hbm), custom_call_target="tpu_custom_call" | custom-call | flops 67108864 | bytes 1310720 | tf_op jit(solution)/shard_map/pallas_call | solution.py:374

commit v6 on v5

--- a/solution.py
+++ b/solution.py
@@ -43,11 +43,14 @@
     return [event for _, _, event in sorted(keyed)]
 
 
+ROUNDS = [("s", 1, 1), ("s", 2, 0), ("s", 3, 0)]
+
+
 def kernel(
     four_hbm, quad_hbm, leaf_hbm, fac_hbm, spars_hbm, root_hbm, order_hbm, part_hbm, coef_hbm, pick_hbm,
     four, quad, leaf, fac, spars, root, order,
     state, partner, own, perm, send_buf, recv_buf, order_col, pick, coef, coef_t, part,
-    in_sem, small_sem, root_sem, out_sem, send_sem, recv_sem, a2a_send_sem, a2a_recv_sem,
+    in_sem, small_sem, root_sem, out_sem, send_sem, recv_sem, a2a_send_sem, a2a_recv_sem, round_sem,
 ):
     me_o = lax.axis_index("order")
     me_l = lax.axis_index("lat")
@@ -71,13 +74,31 @@
     for copy in (all_loads[0][0], all_loads[0][1], small[0]):
         copy.start()
 
+    x, y = me_o // 4, lax.rem(me_o, 4)
+    z, core = me_l // 2, lax.rem(me_l, 2)
+
+    def around(axis):
+        places = []
+        for step in (1, -1):
+            if axis == "x":
+                places.append((lax.rem(x + step + 4, 4) * 4 + y, me_l))
+            elif axis == "y":
+                places.append((x * 4 + lax.rem(y + step + 4, 4), me_l))
+            else:
+                places.append((me_o, lax.rem(z + step + 8, 8) * 2 + core))
+        return places
+
     barrier = pltpu.get_barrier_semaphore()
-    for peer in peers:
-        pl.semaphore_signal(barrier, inc=1, device_id=(me_o, peer), device_id_type=MESH)
-    for i in range(1, N_ORDER):
-        pl.semaphore_signal(
-            barrier, inc=1, device_id=(lax.rem(me_o + i, N_ORDER), me_l), device_id_type=MESH
-        )
+    neighbours = [(me_o, peers[0])] + around("x") + around("y") + around("z")
+    for place in neighbours:
+        pl.semaphore_signal(barrier, inc=1, device_id=place, device_id_type=MESH)
+
+    def tell(n):
+        for place in around("y" if n == 0 else "x") + around("z"):
+            pl.semaphore_signal(round_sem.at[n], inc=1, device_id=place, device_id_type=MESH)
+
+    def hear(n):
+        pl.semaphore_wait(round_sem.at[n], 4)
 
     for c in range(1, CHUNKS):
         for copy in all_loads[c][:2]:
@@ -257,13 +278,19 @@
             c = event[2]
             start_event(c)
             if not passed:
-                pl.semaphore_wait(barrier, LEVELS + N_ORDER - 1)
+                pl.semaphore_wait(barrier, len(neighbours))
                 passed = True
             level_copy(0, c).start()
+            if c == 0:
+                tell(0)
         elif event[0] == "s":
             _, k, c = event
             if event == ("s", 1, 0):
                 small[1].wait()
+            if event in ROUNDS:
+                hear(ROUNDS.index(event))
+                if event != ROUNDS[-1]:
+                    tell(ROUNDS.index(event) + 1)
             if k == 1:
                 all_loads[c][2].wait()
                 own_terms(0, c)
@@ -355,6 +382,7 @@
             pltpu.SemaphoreType.DMA((LEVELS, CHUNKS)),
             pltpu.SemaphoreType.DMA((len(GROUPS),)),
             pltpu.SemaphoreType.DMA((len(GROUPS), 2)),
+            pltpu.SemaphoreType.REGULAR((3,)),
         ],
         compiler_params=pltpu.CompilerParams(
             collective_id=0, has_side_effects=True, vmem_limit_bytes=60 * 1024 * 1024

time: 50.1 us -> 49.3 us (0.984)
  Pallas kernels: 49.7 us -> 49.1 us
    pallas_call x1, Pallas kernels: 47.5 us -> 46.9 us  [per_device(): pl.pallas_call(kernel, out_shape=[jax.ShapeDtypeStruct((512, 512), BF16),...]
where the time goes in v6:
time: 49.3 us; the launch traced here: 49.1 us
  Pallas kernels  49.1 us (100%)
    pallas_call x1, Pallas kernels, per_device(): pl.pallas_call(kernel, out_shape=[jax.ShapeDtypeStruct((512, 512), BF16),...  46.9 us
    pallas_call x1, Pallas kernels, per_device(): pl.pallas_call(finish_kernel, out_shape=jax.ShapeDtypeStruct((2, 2, 128,...  2.2 us

profile of v6, /device:TPU:8, one launch (start us, length us, event | category | flops | bytes accessed | tf_op | source)
XLA Modules:
  0.0 49.1 jit_solution(3415990151383975519)
XLA Ops:
  0.0 46.9 %shard_map.73 = (bf16[512,512]{1,0:T(8,128)(2,1)}, bf16[4,128,128]{2,1,0:T(8,128)(2,1)}, bf16[128,512]{1,0:T(8,128)(2,1)}) custom-call(bf16[32,64,128]{2,1,0:T(8,128)(2,1)} %four_hbm.1, f32[1,128]{1,0:T(1,128)} %bitcast.5, bf16[32,64,128]{2,1,0:T(8,128)(2,1)} %leaf_hbm.1, bf16[32,4,2,1,64,64]{5,4,3,2,1,0:T(8,128)(2,1)} %fac_hbm.1, s32[4,1,32]{2,1,0:T(1,128)} %bitcast.3, ...), custom_call_target="tpu_custom_call" | custom-call | flops 2000000000 | bytes 15000000 | tf_op jit(solution)/shard_map/pallas_call | solution.py:349
  46.9 2.2 %shard_map.74 = bf16[2,2,128,512]{3,2,1,0:T(8,128)(2,1)} custom-call(bf16[512,512]{1,0:T(8,128)(2,1)} %get-tuple-element.8.part_hbm, bf16[4,128,128]{2,1,0:T(8,128)(2,1)} %get-tuple-element.9.coef_hbm, bf16[128,512]{1,0:T(8,128)(2,1)} %get-tuple-element.10.pick_hbm), custom_call_target="tpu_custom_call" | custom-call | flops 67108864 | bytes 1310720 | tf_op jit(solution)/shard_map/pallas_call | solution.py:402

commit v7 on v5

--- a/solution.py
+++ b/solution.py
@@ -43,11 +43,14 @@
     return [event for _, _, event in sorted(keyed)]
 
 
+ROUNDS = [("s", 2, c) for c in range(3, 8)]
+
+
 def kernel(
     four_hbm, quad_hbm, leaf_hbm, fac_hbm, spars_hbm, root_hbm, order_hbm, part_hbm, coef_hbm, pick_hbm,
     four, quad, leaf, fac, spars, root, order,
     state, partner, own, perm, send_buf, recv_buf, order_col, pick, coef, coef_t, part,
-    in_sem, small_sem, root_sem, out_sem, send_sem, recv_sem, a2a_send_sem, a2a_recv_sem,
+    in_sem, small_sem, root_sem, out_sem, send_sem, recv_sem, a2a_send_sem, a2a_recv_sem, near_sem, column_sem, order_sem, round_sem, told_sem,
 ):
     me_o = lax.axis_index("order")
     me_l = lax.axis_index("lat")
@@ -71,13 +74,93 @@
     for copy in (all_loads[0][0], all_loads[0][1], small[0]):
         copy.start()
 
+    z, core = me_l // 2, lax.rem(me_l, 2)
+    bottom = z == 0
+    low_bit = [lax.rem(me_l // (1 << k), 2) == 0 for k in range(LEVELS)]
+    order_low = [lax.rem(me_o // (1 << i), 2) == 0 for i in range(4)]
+    order_peers = [(me_o ^ (1 << i), me_l) for i in range(4)]
+    far_z = (3, 5, 6, 7)
+
+    def signal(sem, place):
+        pl.semaphore_signal(sem, inc=1, device_id=place, device_id_type=MESH)
+
+    def upper(flag):
+        return jnp.logical_not(flag).astype(I32)
+
     barrier = pltpu.get_barrier_semaphore()
-    for peer in peers:
-        pl.semaphore_signal(barrier, inc=1, device_id=(me_o, peer), device_id_type=MESH)
-    for i in range(1, N_ORDER):
-        pl.semaphore_signal(
-            barrier, inc=1, device_id=(lax.rem(me_o + i, N_ORDER), me_l), device_id_type=MESH
-        )
+    signal(barrier, (me_o, peers[0]))
+    for k in range(1, LEVELS):
+
+        @pl.when(low_bit[k])
+        def _():
+            signal(barrier, (me_o, peers[k]))
+
+    @pl.when(bottom)
+    def _():
+        for far in far_z:
+            signal(barrier, (me_o, far * 2 + core))
+        for i in range(4):
+
+            @pl.when(order_low[i])
+            def _():
+                signal(barrier, order_peers[i])
+
+    bits = sum(upper(low_bit[k]) for k in range(1, LEVELS))
+    order_bits = sum(upper(order_low[i]) for i in range(4))
+    expected = (
+        1 + bits + (bits >= 2).astype(I32) + jnp.where(bottom, order_bits, jnp.zeros_like(order_bits))
+    )
+
+    def enter():
+        pl.semaphore_wait(barrier, expected)
+
+    def answer():
+        for k in range(1, LEVELS):
+
+            @pl.when(jnp.logical_not(low_bit[k]))
+            def _():
+                signal(near_sem.at[k], (me_o, peers[k]))
+
+        @pl.when(jnp.logical_not(bottom))
+        def _():
+            signal(column_sem, (me_o, core))
+
+        @pl.when(bottom)
+        def _():
+            for i in range(4):
+
+                @pl.when(jnp.logical_not(order_low[i]))
+                def _():
+                    signal(order_sem.at[i], order_peers[i])
+
+    def hear(k):
+        @pl.when(low_bit[k])
+        def _():
+            pl.semaphore_wait(near_sem.at[k], 1)
+
+    def order_round(n):
+        @pl.when(bottom)
+        def _():
+            if n == 0:
+                pl.semaphore_wait(column_sem, 7)
+                for i in range(4):
+
+                    @pl.when(order_low[i])
+                    def _():
+                        pl.semaphore_wait(order_sem.at[i], 1)
+
+            else:
+                pl.semaphore_wait(round_sem.at[n - 1], 1)
+            if n < 4:
+                signal(round_sem.at[n], order_peers[n])
+            else:
+                for up in range(1, 8):
+                    signal(told_sem, (me_o, up * 2 + core))
+
+    def told():
+        @pl.when(jnp.logical_not(bottom))
+        def _():
+            pl.semaphore_wait(told_sem, 1)
 
     for c in range(1, CHUNKS):
         for copy in all_loads[c][:2]:
@@ -257,21 +340,29 @@
             c = event[2]
             start_event(c)
             if not passed:
-                pl.semaphore_wait(barrier, LEVELS + N_ORDER - 1)
+                enter()
                 passed = True
             level_copy(0, c).start()
+            if c == 0:
+                answer()
         elif event[0] == "s":
             _, k, c = event
             if event == ("s", 1, 0):
                 small[1].wait()
+            if event in ROUNDS:
+                order_round(ROUNDS.index(event))
             if k == 1:
                 all_loads[c][2].wait()
                 own_terms(0, c)
             level_event(k - 1, c)
+            if c == 0 and k < LEVELS:
+                hear(k)
             if k < LEVELS:
                 level_copy(k, c).start()
                 own_terms(k, c)
         elif event[0] == "a":
+            if event[1] == 0:
+                told()
             a2a_event(event[1])
         elif event[0] == "p":
             root_copy.start()
@@ -355,6 +446,11 @@
             pltpu.SemaphoreType.DMA((LEVELS, CHUNKS)),
             pltpu.SemaphoreType.DMA((len(GROUPS),)),
             pltpu.SemaphoreType.DMA((len(GROUPS), 2)),
+            pltpu.SemaphoreType.REGULAR((LEVELS,)),
+            pltpu.SemaphoreType.REGULAR,
+            pltpu.SemaphoreType.REGULAR((4,)),
+            pltpu.SemaphoreType.REGULAR((4,)),
+            pltpu.SemaphoreType.REGULAR,
         ],
         compiler_params=pltpu.CompilerParams(
             collective_id=0, has_side_effects=True, vmem_limit_bytes=60 * 1024 * 1024

time: 50.1 us -> 50.6 us (level)
  Pallas kernels: 49.7 us -> 50.5 us
    pallas_call x1, Pallas kernels: 47.5 us -> 48.3 us  [per_device(): pl.pallas_call(kernel, out_shape=[jax.ShapeDtypeStruct((512, 512), BF16),...]
where the time goes in v7:
time: 50.6 us; the launch traced here: 50.5 us
  Pallas kernels  50.5 us (100%)
    pallas_call x1, Pallas kernels, per_device(): pl.pallas_call(kernel, out_shape=[jax.ShapeDtypeStruct((512, 512), BF16),...  48.3 us
    pallas_call x1, Pallas kernels, per_device(): pl.pallas_call(finish_kernel, out_shape=jax.ShapeDtypeStruct((2, 2, 128,...  2.21 us

profile of v7, /device:TPU:8, one launch (start us, length us, event | category | flops | bytes accessed | tf_op | source)
XLA Modules:
  0.0 50.5 jit_solution(15472351600908609354)
XLA Ops:
  0.0 48.3 %shard_map.73 = (bf16[512,512]{1,0:T(8,128)(2,1)}, bf16[4,128,128]{2,1,0:T(8,128)(2,1)}, bf16[128,512]{1,0:T(8,128)(2,1)}) custom-call(bf16[32,64,128]{2,1,0:T(8,128)(2,1)} %four_hbm.1, f32[1,128]{1,0:T(1,128)} %bitcast.5, bf16[32,64,128]{2,1,0:T(8,128)(2,1)} %leaf_hbm.1, bf16[32,4,2,1,64,64]{5,4,3,2,1,0:T(8,128)(2,1)} %fac_hbm.1, s32[4,1,32]{2,1,0:T(1,128)} %bitcast.3, ...), custom_call_target="tpu_custom_call" | custom-call | flops 2000000000 | bytes 15000000 | tf_op jit(solution)/shard_map/pallas_call | solution.py:413
  48.3 2.2 %shard_map.74 = bf16[2,2,128,512]{3,2,1,0:T(8,128)(2,1)} custom-call(bf16[512,512]{1,0:T(8,128)(2,1)} %get-tuple-element.8.part_hbm, bf16[4,128,128]{2,1,0:T(8,128)(2,1)} %get-tuple-element.9.coef_hbm, bf16[128,512]{1,0:T(8,128)(2,1)} %get-tuple-element.10.pick_hbm), custom_call_target="tpu_custom_call" | custom-call | flops 67108864 | bytes 1310720 | tf_op jit(solution)/shard_map/pallas_call | solution.py:470

commit v8 on v7

--- a/solution.py
+++ b/solution.py
@@ -21,6 +21,7 @@
 LAST = len(GROUPS) - 1
 N_ORDER = 16
 RANK = 64
+HUB = 6
 
 
 HOPS = [(0, 1, 2, 1)[k >> 2] + (0, 1, 2, 1)[k & 3] for k in range(N_ORDER)]
@@ -50,7 +51,7 @@
     four_hbm, quad_hbm, leaf_hbm, fac_hbm, spars_hbm, root_hbm, order_hbm, part_hbm, coef_hbm, pick_hbm,
     four, quad, leaf, fac, spars, root, order,
     state, partner, own, perm, send_buf, recv_buf, order_col, pick, coef, coef_t, part,
-    in_sem, small_sem, root_sem, out_sem, send_sem, recv_sem, a2a_send_sem, a2a_recv_sem, near_sem, column_sem, order_sem, round_sem, told_sem,
+    in_sem, small_sem, root_sem, out_sem, send_sem, recv_sem, a2a_send_sem, a2a_recv_sem, near_sem, order_sem, round_sem, told_sem,
 ):
     me_o = lax.axis_index("order")
     me_l = lax.axis_index("lat")
@@ -75,11 +76,11 @@
         copy.start()
 
     z, core = me_l // 2, lax.rem(me_l, 2)
-    bottom = z == 0
+    hub = z == HUB
     low_bit = [lax.rem(me_l // (1 << k), 2) == 0 for k in range(LEVELS)]
     order_low = [lax.rem(me_o // (1 << i), 2) == 0 for i in range(4)]
     order_peers = [(me_o ^ (1 << i), me_l) for i in range(4)]
-    far_z = (3, 5, 6, 7)
+    far_z = [low for low in range(HUB) if HUB ^ low not in (1, 2, 4)]
 
     def signal(sem, place):
         pl.semaphore_signal(sem, inc=1, device_id=place, device_id_type=MESH)
@@ -95,10 +96,14 @@
         def _():
             signal(barrier, (me_o, peers[k]))
 
-    @pl.when(bottom)
+    for low in far_z:
+
+        @pl.when(z == low)
+        def _():
+            signal(barrier, (me_o, HUB * 2 + core))
+
+    @pl.when(hub)
     def _():
-        for far in far_z:
-            signal(barrier, (me_o, far * 2 + core))
         for i in range(4):
 
             @pl.when(order_low[i])
@@ -107,9 +112,7 @@
 
     bits = sum(upper(low_bit[k]) for k in range(1, LEVELS))
     order_bits = sum(upper(order_low[i]) for i in range(4))
-    expected = (
-        1 + bits + (bits >= 2).astype(I32) + jnp.where(bottom, order_bits, jnp.zeros_like(order_bits))
-    )
+    expected = 1 + bits + hub.astype(I32) * (order_bits + len(far_z))
 
     def enter():
         pl.semaphore_wait(barrier, expected)
@@ -121,11 +124,7 @@
             def _():
                 signal(near_sem.at[k], (me_o, peers[k]))
 
-        @pl.when(jnp.logical_not(bottom))
-        def _():
-            signal(column_sem, (me_o, core))
-
-        @pl.when(bottom)
+        @pl.when(hub)
         def _():
             for i in range(4):
 
@@ -139,10 +138,9 @@
             pl.semaphore_wait(near_sem.at[k], 1)
 
     def order_round(n):
-        @pl.when(bottom)
+        @pl.when(hub)
         def _():
             if n == 0:
-                pl.semaphore_wait(column_sem, 7)
                 for i in range(4):
 
                     @pl.when(order_low[i])
@@ -154,11 +152,12 @@
             if n < 4:
                 signal(round_sem.at[n], order_peers[n])
             else:
-                for up in range(1, 8):
-                    signal(told_sem, (me_o, up * 2 + core))
+                for other in range(8):
+                    if other != HUB:
+                        signal(told_sem, (me_o, other * 2 + core))
 
     def told():
-        @pl.when(jnp.logical_not(bottom))
+        @pl.when(jnp.logical_not(hub))
         def _():
             pl.semaphore_wait(told_sem, 1)
 
@@ -447,7 +446,6 @@
             pltpu.SemaphoreType.DMA((len(GROUPS),)),
             pltpu.SemaphoreType.DMA((len(GROUPS), 2)),
             pltpu.SemaphoreType.REGULAR((LEVELS,)),
-            pltpu.SemaphoreType.REGULAR,
             pltpu.SemaphoreType.REGULAR((4,)),
             pltpu.SemaphoreType.REGULAR((4,)),
             pltpu.SemaphoreType.REGULAR,

time: 50.6 us -> 50.6 us (level)
  no operation moved by 1% of the time
where the time goes in v8:
time: 50.6 us; the launch traced here: 50.5 us
  Pallas kernels  50.5 us (100%)
    pallas_call x1, Pallas kernels, per_device(): pl.pallas_call(kernel, out_shape=[jax.ShapeDtypeStruct((512, 512), BF16),...  48.3 us
    pallas_call x1, Pallas kernels, per_device(): pl.pallas_call(finish_kernel, out_shape=jax.ShapeDtypeStruct((2, 2, 128,...  2.21 us

profile of v8, /device:TPU:8, one launch (start us, length us, event | category | flops | bytes accessed | tf_op | source)
XLA Modules:
  0.0 50.5 jit_solution(16400833913245582572)
XLA Ops:
  0.0 48.3 %shard_map.73 = (bf16[512,512]{1,0:T(8,128)(2,1)}, bf16[4,128,128]{2,1,0:T(8,128)(2,1)}, bf16[128,512]{1,0:T(8,128)(2,1)}) custom-call(bf16[32,64,128]{2,1,0:T(8,128)(2,1)} %four_hbm.1, f32[1,128]{1,0:T(1,128)} %bitcast.5, bf16[32,64,128]{2,1,0:T(8,128)(2,1)} %leaf_hbm.1, bf16[32,4,2,1,64,64]{5,4,3,2,1,0:T(8,128)(2,1)} %fac_hbm.1, s32[4,1,32]{2,1,0:T(1,128)} %bitcast.3, ...), custom_call_target="tpu_custom_call" | custom-call | flops 2000000000 | bytes 15000000 | tf_op jit(solution)/shard_map/pallas_call | solution.py:412
  48.3 2.2 %shard_map.74 = bf16[2,2,128,512]{3,2,1,0:T(8,128)(2,1)} custom-call(bf16[512,512]{1,0:T(8,128)(2,1)} %get-tuple-element.8.part_hbm, bf16[4,128,128]{2,1,0:T(8,128)(2,1)} %get-tuple-element.9.coef_hbm, bf16[128,512]{1,0:T(8,128)(2,1)} %get-tuple-element.10.pick_hbm), custom_call_target="tpu_custom_call" | custom-call | flops 67108864 | bytes 1310720 | tf_op jit(solution)/shard_map/pallas_call | solution.py:468

commit v9 on v6

--- a/solution.py
+++ b/solution.py
@@ -33,17 +33,18 @@
     for c in range(CHUNKS):
         keyed.append((c * 1.0, 0, ("s", 0, c)))
         keyed.append((c * 1.0 + 2.5, 1, ("s", 1, c)))
-        keyed.append((c * 1.0 + 5.5, 2, ("s", 2, c)))
+        keyed.append((c * 1.5 + 5.5, 2, ("s", 2, c)))
         keyed.append((c * 2.0 + 12.0, 3, ("s", 3, c)))
-        keyed.append((c * 2.0 + 18.5, 4, ("s", 4, c)))
+        keyed.append((c * 2.0 + 15.65, 4, ("d", c)))
+        keyed.append((c * 2.0 + 19.5, 4, ("s", 4, c)))
     for g, chunks in enumerate(GROUPS):
-        keyed.append((chunks[-1] * 2.0 + 18.6, 5, ("a", g)))
+        keyed.append((chunks[-1] * 2.0 + 19.6, 5, ("a", g)))
         keyed.append((999 + g, 6, ("r", g)))
     keyed.append((8.1, 7, ("p",)))
     return [event for _, _, event in sorted(keyed)]
 
 
-ROUNDS = [("s", 1, 1), ("s", 2, 0), ("s", 3, 0)]
+ROUNDS = [("s", 2, 0), ("s", 2, 2), ("s", 3, 0)]
 
 
 def kernel(
@@ -273,6 +274,7 @@
 
     small[0].wait()
     passed = False
+    hold = (z == 1) | (z == 2)
     for event in schedule():
         if event[0] == "s" and event[1] == 0:
             c = event[2]
@@ -295,9 +297,14 @@
                 all_loads[c][2].wait()
                 own_terms(0, c)
             level_event(k - 1, c)
-            if k < LEVELS:
+            if k == LEVELS - 1:
+                pl.when(jnp.logical_not(hold))(level_copy(k, c).start)
+                own_terms(k, c)
+            elif k < LEVELS:
                 level_copy(k, c).start()
                 own_terms(k, c)
+        elif event[0] == "d":
+            pl.when(hold)(level_copy(LEVELS - 1, event[1]).start)
         elif event[0] == "a":
             a2a_event(event[1])
         elif event[0] == "p":

time: 49.3 us -> 48.1 us (0.976)
  Pallas kernels: 49.1 us -> 48 us
    pallas_call x1, Pallas kernels: 46.9 us -> 45.8 us  [per_device(): pl.pallas_call(kernel, out_shape=[jax.ShapeDtypeStruct((512, 512), BF16),...]
where the time goes in v9:
time: 48.1 us; the launch traced here: 48 us
  Pallas kernels  48 us (100%)
    pallas_call x1, Pallas kernels, per_device(): pl.pallas_call(kernel, out_shape=[jax.ShapeDtypeStruct((512, 512), BF16),...  45.8 us
    pallas_call x1, Pallas kernels, per_device(): pl.pallas_call(finish_kernel, out_shape=jax.ShapeDtypeStruct((2, 2, 128,...  2.2 us

profile of v9, /device:TPU:8, one launch (start us, length us, event | category | flops | bytes accessed | tf_op | source)
XLA Modules:
  0.0 48.0 jit_solution(3153479969899383330)
XLA Ops:
  0.0 45.8 %shard_map.73 = (bf16[512,512]{1,0:T(8,128)(2,1)}, bf16[4,128,128]{2,1,0:T(8,128)(2,1)}, bf16[128,512]{1,0:T(8,128)(2,1)}) custom-call(bf16[32,64,128]{2,1,0:T(8,128)(2,1)} %four_hbm.1, f32[1,128]{1,0:T(1,128)} %bitcast.5, bf16[32,64,128]{2,1,0:T(8,128)(2,1)} %leaf_hbm.1, bf16[32,4,2,1,64,64]{5,4,3,2,1,0:T(8,128)(2,1)} %fac_hbm.1, s32[4,1,32]{2,1,0:T(1,128)} %bitcast.3, ...), custom_call_target="tpu_custom_call" | custom-call | flops 2000000000 | bytes 15000000 | tf_op jit(solution)/shard_map/pallas_call | solution.py:356
  45.8 2.2 %shard_map.74 = bf16[2,2,128,512]{3,2,1,0:T(8,128)(2,1)} custom-call(bf16[512,512]{1,0:T(8,128)(2,1)} %get-tuple-element.8.part_hbm, bf16[4,128,128]{2,1,0:T(8,128)(2,1)} %get-tuple-element.9.coef_hbm, bf16[128,512]{1,0:T(8,128)(2,1)} %get-tuple-element.10.pick_hbm), custom_call_target="tpu_custom_call" | custom-call | flops 67108864 | bytes 1310720 | tf_op jit(solution)/shard_map/pallas_call | solution.py:409

commit v10 on v9

--- a/solution.py
+++ b/solution.py
@@ -33,7 +33,7 @@
     for c in range(CHUNKS):
         keyed.append((c * 1.0, 0, ("s", 0, c)))
         keyed.append((c * 1.0 + 2.5, 1, ("s", 1, c)))
-        keyed.append((c * 1.5 + 5.5, 2, ("s", 2, c)))
+        keyed.append((c * 1.25 + 5.5, 2, ("s", 2, c)))
         keyed.append((c * 2.0 + 12.0, 3, ("s", 3, c)))
         keyed.append((c * 2.0 + 15.65, 4, ("d", c)))
         keyed.append((c * 2.0 + 19.5, 4, ("s", 4, c)))

time: 48.1 us -> 47.8 us (level)
  no operation moved by 1% of the time
where the time goes in v10:
time: 47.8 us; the launch traced here: 47.7 us
  Pallas kernels  47.7 us (100%)
    pallas_call x1, Pallas kernels, per_device(): pl.pallas_call(kernel, out_shape=[jax.ShapeDtypeStruct((512, 512), BF16),...  45.5 us
    pallas_call x1, Pallas kernels, per_device(): pl.pallas_call(finish_kernel, out_shape=jax.ShapeDtypeStruct((2, 2, 128,...  2.2 us

profile of v10, /device:TPU:8, one launch (start us, length us, event | category | flops | bytes accessed | tf_op | source)
XLA Modules:
  0.0 47.7 jit_solution(2303357555798508632)
XLA Ops:
  0.0 45.5 %shard_map.73 = (bf16[512,512]{1,0:T(8,128)(2,1)}, bf16[4,128,128]{2,1,0:T(8,128)(2,1)}, bf16[128,512]{1,0:T(8,128)(2,1)}) custom-call(bf16[32,64,128]{2,1,0:T(8,128)(2,1)} %four_hbm.1, f32[1,128]{1,0:T(1,128)} %bitcast.5, bf16[32,64,128]{2,1,0:T(8,128)(2,1)} %leaf_hbm.1, bf16[32,4,2,1,64,64]{5,4,3,2,1,0:T(8,128)(2,1)} %fac_hbm.1, s32[4,1,32]{2,1,0:T(1,128)} %bitcast.3, ...), custom_call_target="tpu_custom_call" | custom-call | flops 2000000000 | bytes 15000000 | tf_op jit(solution)/shard_map/pallas_call | solution.py:356
  45.5 2.2 %shard_map.74 = bf16[2,2,128,512]{3,2,1,0:T(8,128)(2,1)} custom-call(bf16[512,512]{1,0:T(8,128)(2,1)} %get-tuple-element.8.part_hbm, bf16[4,128,128]{2,1,0:T(8,128)(2,1)} %get-tuple-element.9.coef_hbm, bf16[128,512]{1,0:T(8,128)(2,1)} %get-tuple-element.10.pick_hbm), custom_call_target="tpu_custom_call" | custom-call | flops 67108864 | bytes 1310720 | tf_op jit(solution)/shard_map/pallas_call | solution.py:409

commit v11 on v9

--- a/solution.py
+++ b/solution.py
@@ -326,19 +326,24 @@
     copies = [
         pltpu.make_async_copy(coef_hbm, coef_t, in_sem.at[0]),
         pltpu.make_async_copy(pick_hbm, pick, in_sem.at[1]),
-        pltpu.make_async_copy(part_hbm, part, in_sem.at[2]),
+    ] + [
+        pltpu.make_async_copy(
+            part_hbm.at[pl.ds(cc * 128, 128)], part.at[pl.ds(cc * 128, 128)], in_sem.at[2 + cc]
+        )
+        for cc in range(4)
     ]
     for copy in copies:
         copy.start()
     degree = lax.axis_index("lat") * 128 + lax.broadcasted_iota(I32, (128, 512), 0)
     window = DEGREES // 512 * lax.broadcasted_iota(I32, (128, 512), 1)
     alive = degree >= window
-    for copy in copies:
+    for copy in copies[:2]:
         copy.wait()
     natural = jnp.dot(coef_t[...].reshape(512, 128), pick[...], preferred_element_type=F32)
     out_copies = []
     for cc in range(4):
         rows = slice(cc * 128, (cc + 1) * 128)
+        copies[2 + cc].wait()
         total = part[rows].astype(F32) + natural[rows]
         out[cc] = jnp.where(alive, total, 0.0).astype(BF16)
         copy = pltpu.make_async_copy(out.at[cc], out_hbm.at[cc // 2, cc % 2], out_sem.at[cc])
@@ -416,7 +421,7 @@
             vmem((4, 128, 128), BF16),
             vmem((128, 512), BF16),
             vmem((4, 128, 512), BF16),
-            pltpu.SemaphoreType.DMA((3,)),
+            pltpu.SemaphoreType.DMA((6,)),
             pltpu.SemaphoreType.DMA((4,)),
         ],
         compiler_params=pltpu.CompilerParams(vmem_limit_bytes=60 * 1024 * 1024),

time: 48.1 us -> 48 us (level)
  no operation moved by 1% of the time
where the time goes in v11:
time: 48 us; the launch traced here: 47.9 us
  Pallas kernels  47.9 us (100%)
    pallas_call x1, Pallas kernels, per_device(): pl.pallas_call(kernel, out_shape=[jax.ShapeDtypeStruct((512, 512), BF16),...  45.8 us
    pallas_call x1, Pallas kernels, per_device(): pl.pallas_call(finish_kernel, out_shape=jax.ShapeDtypeStruct((2, 2, 128,...  2.15 us

profile of v11, /device:TPU:8, one launch (start us, length us, event | category | flops | bytes accessed | tf_op | source)
XLA Modules:
  0.0 47.9 jit_solution(17846556223752816337)
XLA Ops:
  0.0 45.8 %shard_map.73 = (bf16[512,512]{1,0:T(8,128)(2,1)}, bf16[4,128,128]{2,1,0:T(8,128)(2,1)}, bf16[128,512]{1,0:T(8,128)(2,1)}) custom-call(bf16[32,64,128]{2,1,0:T(8,128)(2,1)} %four_hbm.1, f32[1,128]{1,0:T(1,128)} %bitcast.5, bf16[32,64,128]{2,1,0:T(8,128)(2,1)} %leaf_hbm.1, bf16[32,4,2,1,64,64]{5,4,3,2,1,0:T(8,128)(2,1)} %fac_hbm.1, s32[4,1,32]{2,1,0:T(1,128)} %bitcast.3, ...), custom_call_target="tpu_custom_call" | custom-call | flops 2000000000 | bytes 15000000 | tf_op jit(solution)/shard_map/pallas_call | solution.py:361
  45.8 2.2 %shard_map.74 = bf16[2,2,128,512]{3,2,1,0:T(8,128)(2,1)} custom-call(bf16[512,512]{1,0:T(8,128)(2,1)} %get-tuple-element.8.part_hbm, bf16[4,128,128]{2,1,0:T(8,128)(2,1)} %get-tuple-element.9.coef_hbm, bf16[128,512]{1,0:T(8,128)(2,1)} %get-tuple-element.10.pick_hbm), custom_call_target="tpu_custom_call" | custom-call | flops 67108864 | bytes 1310720 | tf_op jit(solution)/shard_map/pallas_call | solution.py:414
